TPU v7x, 128 devices: a whole 4x4x4 slice. The times are simulated.
128 devices in a mesh: space: 32 (over x, y, core), dir: 4 (over z).
Axes of the slice: x: 4, y: 4, z: 4, core: 2. Of those that a mesh axis runs over, the one named last changes fastest.
Arguments:
- currents: bfloat16 [1024, 2, 32, 256], P('space'), may hold values from -6 to 6
- near_blocks: bfloat16 [1024, 6, 2, 256, 256], P('space', None, None, 'dir'), may hold values from -0.15625 to 0.15625
- near_list: int32 [1024, 6], P('space'), may hold values from 0 to 1023, as said below
- near_count: int32 [1024], P('space'), may hold values from 3 to 6, as said below
- radiate: bfloat16 [1024, 2, 128, 256], P('space', None, 'dir'), may hold values from -0.375 to 0.375
- receive: float32 [1024, 2, 128, 256], P('space', None, 'dir'), may hold values from -0.0625 to 0.0625
- phase_one: float32 [4, 512], replicated, may hold values from -3.140625 to 3.140625
- phase_two: float32 [4, 2048], replicated, may hold values from -3.140625 to 3.140625
- interp_one: float32 [512, 128], replicated, may hold values from -0.5 to 0.5
- interp_two: float32 [2048, 512], replicated, may hold values from -0.25 to 0.25
- trans_one: float32 [40, 2, 512], P(None, None, 'dir'), may hold values from -2 to 2
- kind_one: int32 [256, 8], P('space'), may hold values from 0 to 39
- list_one: int32 [256, 8], P('space'), may hold values from 0 to 255, as said below
- trans_two: float32 [40, 2, 2048], P(None, None, 'dir'), may hold values from -2 to 2
- kind_two: int32 [64, 8], replicated, may hold values from 0 to 39
- list_two: int32 [64, 8], replicated, may hold values from 0 to 63
Outputs:
- fields: float32 [1024, 2, 32, 256], P('space', None, None, 'dir')
Inputs may be any that keep to these rules, and one draw needn't show every extreme that they name: `near_list`: row b names box b in slot 0, the box exactly 32 below b in slot 1 (above, for b < 32) and the box exactly 32 above b in slot 2 (below, for the last 32 boxes); every entry lies within 32 boxes of b. `near_count`: box 0 uses all slots. `list_one`: every entry of row p lies within 8 parents of p, and slot 0 exactly 8 away.
All inputs are finite; a program needn't handle non-finite values.
Results may differ from a plain program's by a relative error of at most 0.0018.
Values may be sent and summed in bfloat16 or wider, within the bound.
No kernel may reach another device: no remote copies, remote signals or barrier semaphores. Data moves between devices by JAX's collectives and lax.ppermute only.
A program may use at most 128 MiB of HBM per device.

v0:
```python
import jax
import jax.numpy as jnp
from jax import lax
from jax.experimental import pallas as pl
from jax.experimental.pallas import tpu as pltpu
from jax.sharding import PartitionSpec as P

F32 = jnp.float32
BF16 = jnp.bfloat16
I32 = jnp.int32
I16 = jnp.int16
IN_HBM = pl.BlockSpec(memory_space=pltpu.HBM)
ANYWHERE = pl.BlockSpec(memory_space=pl.ANY)
MIB = 1024 * 1024
SMALL = 2**12
LARGE = 2**36


def call(kernel, outs, operands, scratch, copies, cost, name, landed=(), limit=52):
    shapes = tuple(jax.ShapeDtypeStruct(shape, kind) for shape, kind in outs)
    return pl.pallas_call(
        kernel,
        out_shape=shapes,
        in_specs=[ANYWHERE if n in landed else IN_HBM for n in range(len(operands))],
        out_specs=tuple(IN_HBM for _ in outs),
        scratch_shapes=[*scratch, pltpu.SemaphoreType.DMA((copies,))],
        compiler_params=pltpu.CompilerParams(vmem_limit_bytes=limit * MIB),
        cost_estimate=pl.CostEstimate(flops=cost, bytes_accessed=cost, transcendentals=0),
        name=name,
    )(*operands)


def begin(sems, *pairs, first=0):
    copies = [pltpu.make_async_copy(source, target, sems.at[first + n]) for n, (source, target) in enumerate(pairs)]
    for copy in copies:
        copy.start()
    return copies


def finish(*copies):
    for copy in copies:
        copy.wait()


def rows_by_rows(a, b):
    return lax.dot_general(a, b, (((1,), (1,)), ((), ())), preferred_element_type=F32)


def rows_by_cols(a, b):
    return lax.dot_general(a, b, (((1,), (0,)), ((), ())), preferred_element_type=F32)


def halves(x):
    high = x.astype(BF16)
    return high, (x - high.astype(F32)).astype(BF16)


def product(dot, x, high, low):
    x_high, x_low = halves(x)
    return dot(x_high, high) + (dot(x_high, low) + dot(x_low, high))


def lanes_of(shape):
    return lax.broadcasted_iota(I32, shape, len(shape) - 1)


def swap_half(x):
    return pltpu.roll(x, 64, x.ndim - 1)


def sender(k):
    return lax.rem(lax.axis_index("dir") + 4 - k, 4)


def receiver(k):
    return lax.rem(lax.axis_index("dir") + k, 4)


def power_of(largest):
    return jnp.ceil(jnp.log2(jnp.maximum(largest, 2.0**-100)))


def code_of(scaled):
    return jnp.round(scaled).astype(I32).astype(I16)


def value_of(code):
    return code.astype(I32).astype(F32)


def scale_from(power):
    return jnp.exp2(-power) * 32767.0


def unit_from(power):
    return jnp.exp2(power) * (1.0 / 32767.0)


def unit_of(rows):
    return unit_from(value_of(rows)[0:1])


def leaf_kernel(cur_from, rad_from, one_from, two_from, out0, out1, out2, out3, cur, rad, one, trans, held, codes, sems):
    near_half, far_half = slice(0, 16), slice(16, 32)
    copies = begin(
        sems,
        (cur_from.at[near_half], cur.at[near_half]),
        (rad_from.at[near_half], rad.at[near_half]),
        (cur_from.at[far_half], cur.at[far_half]),
        (rad_from.at[far_half], rad.at[far_half]),
        (one_from, one),
        (two_from, trans),
    )
    lane = lanes_of((32, 128)) // 32
    for p in range(8):
        if p == 0:
            finish(*copies[0:2])
        if p == 4:
            finish(*copies[2:4])
        boxes = cur[4 * p : 4 * p + 4].reshape(256, 256)
        re_rows = rad[4 * p : 4 * p + 4, 0].reshape(128, 256)
        im_rows = rad[4 * p : 4 * p + 4, 1].reshape(128, 256)
        with_re = rows_by_rows(boxes, re_rows)
        with_im = rows_by_rows(boxes, im_rows)
        re = jnp.zeros((32, 128), F32)
        im = jnp.zeros((32, 128), F32)
        for j in range(4):
            a = with_re[64 * j : 64 * j + 64]
            b = with_im[64 * j : 64 * j + 64]
            re = jnp.where(lane == j, a[:32] - b[32:], re)
            im = jnp.where(lane == j, a[32:] + b[:32], im)
        for e in range(4):
            held[e, 16 * p : 16 * p + 8] = re[8 * e : 8 * e + 8]
            held[e, 16 * p + 8 : 16 * p + 16] = im[8 * e : 8 * e + 8]
    finish(*copies[4:6])
    part = lax.rem(lax.axis_index("space"), 8)
    at = pl.ds(pl.multiple_of(part // 2 * 128, 128), 128)
    odd = part % 2
    re = trans[:, 0, at]
    im = trans[:, 1, at]
    lane = lanes_of((40, 128)) < 64
    even_cut = jnp.where(lane, re, swap_half(im))
    odd_cut = jnp.where(lane, swap_half(re), im)
    cut = jnp.where(odd == 1, odd_cut, even_cut)
    cut = jnp.concatenate([cut, jnp.zeros((8, 128), F32)], axis=0)
    table = jnp.concatenate([one[:, 0, :], one[:, 1, :]], axis=0)
    row = lax.broadcasted_iota(I32, (16, 128), 0)
    powers = jnp.zeros((16, 128), F32)
    coded = []
    for n, values in enumerate((held[...], cut, table)):
        flat = jnp.abs(values).reshape(-1, 128)
        power = power_of(jnp.max(flat, keepdims=True))
        powers = jnp.where(row == n, power, powers)
        coded.append(code_of(values.reshape(-1, 128) * scale_from(power)))
    for e in range(4):
        codes[e, 0:128] = coded[0][128 * e : 128 * e + 128]
        codes[e, 128:176] = coded[1]
        codes[e, 176:256] = coded[2]
        codes[e, 256:272] = powers.astype(I32).astype(I16)
    finish(*begin(sems, *[(codes.at[receiver(k)], out) for k, out in enumerate((out0, out1, out2, out3))]))


def pack_kernel(rec_from, one_from, two_from, *refs):
    outs = refs[:4]
    angles_to = refs[4:8]
    rec, one, two, cos1, sin1, cos2, sin2, held, sems = refs[8:]
    copies = begin(
        sems, (one_from, one), (two_from, two), (rec_from.at[0:16], rec.at[0:16]), (rec_from.at[16:32], rec.at[16:32])
    )
    finish(*copies[0:2])
    cos1[...] = jnp.cos(one[...])
    sin1[...] = jnp.sin(one[...])
    cos2[...] = jnp.cos(two[...])
    sin2[...] = jnp.sin(two[...])
    angle_copies = begin(sems, *zip((cos1, sin1, cos2, sin2), angles_to), first=4)
    largest = jnp.zeros((32, 256), F32)
    for t in range(2):
        finish(copies[2 + t])

        def look(b, found):
            return jnp.maximum(found, jnp.maximum(jnp.abs(rec[b, 0]), jnp.abs(rec[b, 1])))

        largest = lax.fori_loop(16 * t, 16 * t + 16, look, largest, unroll=4)
    power = power_of(jnp.max(largest, keepdims=True))
    unit = scale_from(power)
    for e in range(4):
        held[e, 1024:1040] = jnp.broadcast_to(power, (16, 128)).astype(I32).astype(I16)
    lane = lanes_of((32, 128)) < 64

    def body(b, carry):
        rows = pl.ds(pl.multiple_of(b * 32, 32), 32)
        for m in range(2):
            re = rec[b, 0, :, 128 * m : 128 * m + 128] * unit
            im = rec[b, 1, :, 128 * m : 128 * m + 128] * unit
            held[2 * m, rows, :] = code_of(jnp.where(lane, re, swap_half(im)))
            held[2 * m + 1, rows, :] = code_of(jnp.where(lane, swap_half(re), im))
        return carry

    lax.fori_loop(0, 32, body, 0, unroll=4)
    finish(*begin(sems, *[(held.at[receiver(k)], out) for k, out in enumerate(outs)]), *angle_copies)


def lift_kernel(r0, r1, r2, r3, *refs):
    one_from, two_from, *angles_from = refs[:6]
    parent_to, halo_to, message_to = refs[6:9]
    one, two, cos1, sin1, cos2, sin2 = refs[9:15]
    parent, halo, message, codes, held, top, sems = refs[15:]
    copies = begin(
        sems,
        *[(r, codes.at[sender(k)]) for k, r in enumerate((r0, r1, r2, r3))],
        (one_from, one),
        *zip(angles_from, (cos1, sin1, cos2, sin2)),
        *[(two_from.at[512 * t : 512 * t + 512], two.at[512 * t : 512 * t + 512]) for t in range(4)],
    )
    finish(*copies[0:9])
    for e in range(4):
        held[e] = value_of(codes[e, 0:128]) * unit_of(codes[e, 256:272])
    w1h, w1l = halves(one[...])
    lane = lanes_of((128, 128)) // 32
    rows = []
    for j in range(4):
        x = jnp.zeros((128, 128), F32)
        for e in range(4):
            piece = held[e]
            shift = (32 * (e - j)) % 128
            if shift:
                piece = pltpu.roll(piece, shift, 1)
            x = jnp.where(lane == e, piece, x)
        rows.append(x)
    up = product(rows_by_rows, jnp.concatenate(rows, axis=0), w1h, w1l)
    up = up.reshape(4, 8, 2, 8, 512)
    re = jnp.zeros((8, 8, 512), F32)
    im = jnp.zeros((8, 8, 512), F32)
    for j in range(4):
        c = cos1[j : j + 1, :][None]
        s = sin1[j : j + 1, :][None]
        re = re + (c * up[j, :, 0] - s * up[j, :, 1])
        im = im + (c * up[j, :, 1] + s * up[j, :, 0])
    parent[:, 0] = re
    parent[:, 1] = im
    whole = parent[...].reshape(128, 512)
    halo[...] = whole.astype(BF16)
    copies += begin(sems, (parent, parent_to), (halo, halo_to), first=13)
    x_high, x_low = halves(whole)
    for t in range(4):
        finish(copies[9 + t])
        rows = slice(512 * t, 512 * t + 512)
        high, low = halves(two[rows, :])
        part = rows_by_rows(x_high, high) + (rows_by_rows(x_high, low) + rows_by_rows(x_low, high))
        top[:, :, :, :, rows] = part.reshape(2, 4, 2, 8, 512)
    lane = lanes_of((16, 128)) < 64
    for m in range(16):
        at = slice(128 * m, 128 * m + 128)
        re = jnp.zeros((2, 8, 128), F32)
        im = jnp.zeros((2, 8, 128), F32)
        for j in range(4):
            c = cos2[j : j + 1, at][None]
            s = sin2[j : j + 1, at][None]
            u_re = top[:, j, 0, :, at]
            u_im = top[:, j, 1, :, at]
            re = re + (c * u_re - s * u_im)
            im = im + (c * u_im + s * u_re)
        re = re.reshape(16, 128)
        im = im.reshape(16, 128)
        message[2 * m] = jnp.where(lane, re, swap_half(im))
        message[2 * m + 1] = jnp.where(lane, swap_half(re), im)
    copies += begin(sems, (message, message_to), first=15)
    finish(*copies[13:])


def top_kernel(kinds_from, lists_from, top_from, m0, m1, m2, m3, out_to, kinds, lists, top, cuts, first, second, out, sems):
    finish(
        *begin(
            sems,
            (kinds_from, kinds),
            (lists_from, lists),
            (top_from, top),
            *[(m.at[128:272], cuts.at[sender(k)]) for k, m in enumerate((m0, m1, m2, m3))],
        )
    )
    chosen = lax.axis_index("space") // 8
    unit = unit_from(value_of(cuts[chosen, 128:144])[1:2])
    table = (value_of(cuts[chosen, 0:48]) * unit)[0:40]
    lane = lanes_of((40, 128)) < 64
    turned = swap_half(table)
    first[...] = jnp.where(lane, table, turned)
    second[...] = jnp.where(lane, turned, -table)

    def body(g, carry):
        straight = jnp.zeros((8, 128), F32)
        crossed = jnp.zeros((8, 128), F32)
        for k in range(8):
            kind = kinds[k, g]
            value = top[lists[k, g]]
            straight = straight + first[pl.ds(kind, 1), :] * value
            crossed = crossed + second[pl.ds(kind, 1), :] * value
        out[g] = straight + swap_half(crossed)
        return carry

    lax.fori_loop(0, 64, body, 0, unroll=8)
    finish(*begin(sems, (out, out_to)))


def parent_kernel(
    kinds_from, lists_from, before_from, parent_from, after_from, m0, m1, m2, m3,
    out_to,
    kinds, lists, before, after, held, codes, table, out, sems,
):
    finish(
        *begin(
            sems,
            (kinds_from, kinds),
            (lists_from, lists),
            (before_from, before),
            (parent_from, held.at[8:16]),
            (after_from, after),
            *[(m.at[176:272], codes.at[sender(k)]) for k, m in enumerate((m0, m1, m2, m3))],
        )
    )
    base = lax.axis_index("space") * 8 - 8
    for e in range(4):
        table[e] = value_of(codes[e, 0:80]) * unit_from(value_of(codes[e, 80:96])[2:3])
    held[0:8] = before[...].astype(F32).reshape(8, 2, 8, 512)
    held[16:24] = after[...].astype(F32).reshape(8, 2, 8, 512)

    def body(p, carry):
        re = [jnp.zeros((8, 128), F32) for _ in range(4)]
        im = [jnp.zeros((8, 128), F32) for _ in range(4)]
        for k in range(8):
            kind = kinds[p, k]
            source = lists[p, k] - base
            for m in range(4):
                at = slice(128 * m, 128 * m + 128)
                s_re = held[source, 0, :, at]
                s_im = held[source, 1, :, at]
                c_re = table[m, pl.ds(kind, 1), :]
                c_im = table[m, pl.ds(kind + 40, 1), :]
                re[m] = re[m] + (c_re * s_re - c_im * s_im)
                im[m] = im[m] + (c_re * s_im + c_im * s_re)
        for m in range(4):
            at = slice(128 * m, 128 * m + 128)
            out[p, 0, :, at] = re[m]
            out[p, 1, :, at] = im[m]
        return carry

    lax.fori_loop(0, 8, body, 0)
    finish(*begin(sems, (out, out_to)))


def lower_kernel(arrived_from, near_one_from, *refs):
    sources = refs[:6]
    out_to = refs[6]
    cos1, sin1, cos2, sin2, one, two = refs[7:13]
    arrived, near_one, child_high, child_low, held, out, sems = refs[13:]
    copies = begin(
        sems,
        (arrived_from, arrived),
        (near_one_from, near_one),
        *zip(sources[:5], refs[7:12]),
        *[(sources[5].at[512 * t : 512 * t + 512], two.at[512 * t : 512 * t + 512]) for t in range(4)],
    )
    finish(copies[0], *copies[4:6])
    lane = lanes_of((16, 128)) < 64
    for m in range(16):
        at = slice(128 * m, 128 * m + 128)
        a = arrived[2 * m]
        b = arrived[2 * m + 1]
        re = jnp.where(lane, a, swap_half(b)).reshape(2, 8, 128)
        im = jnp.where(lane, swap_half(a), b).reshape(2, 8, 128)
        for j in range(4):
            c = cos2[j : j + 1, at][None]
            s = sin2[j : j + 1, at][None]
            both = jnp.concatenate([(c * re + s * im)[:, None], (c * im - s * re)[:, None]], axis=1)
            high, low = halves(both.reshape(2, 16, 128))
            for g in range(2):
                rows = slice(64 * g + 16 * j, 64 * g + 16 * j + 16)
                child_high[rows, at] = high[g]
                child_low[rows, at] = low[g]
    local = jnp.zeros((128, 512), F32)
    for t in range(4):
        finish(copies[7 + t])
        at = slice(512 * t, 512 * t + 512)
        high = child_high[:, at]
        w2h, w2l = halves(two[at, :])
        local = local + (rows_by_cols(high, w2h) + (rows_by_cols(high, w2l) + rows_by_cols(child_low[:, at], w2h)))
    finish(*copies[1:4], copies[6])
    w1h, w1l = halves(one[...])
    local = local.reshape(8, 2, 8, 512) + near_one[...]
    re = local[:, 0]
    im = local[:, 1]
    for j in range(4):
        c = cos1[j : j + 1, :][None]
        s = sin1[j : j + 1, :][None]
        both = jnp.concatenate([(c * re + s * im)[:, None], (c * im - s * re)[:, None]], axis=1)
        down = product(rows_by_cols, both.reshape(128, 512), w1h, w1l)
        held[128 * j : 128 * j + 128] = down
    largest = jnp.max(jnp.abs(held[...]), keepdims=True)
    power = power_of(largest)
    out[0:512] = code_of(held[...] * scale_from(power))
    out[512:528] = jnp.broadcast_to(power, (16, 128)).astype(I32).astype(I16)
    finish(*begin(sems, (out, out_to)))


def near_kernel(lists_from, counts_from, before, current, after, blocks_from, out_to, lists, counts, held, blocks, out, sems):
    copies = begin(
        sems,
        (lists_from, lists),
        (counts_from, counts),
        (before, held.at[0:32]),
        (current, held.at[32:64]),
        (after, held.at[64:96]),
        *[(blocks_from.at[4 * t : 4 * t + 4], blocks.at[4 * t : 4 * t + 4]) for t in range(8)],
    )
    held[96] = jnp.zeros((64, 256), BF16)
    finish(*copies[0:5])
    base = lax.axis_index("space") * 32 - 32

    for t in range(8):
        finish(copies[5 + t])

        def body(n, carry):
            for box in (4 * t + 2 * n, 4 * t + 2 * n + 1):
                total = jnp.zeros((64, 128), F32)
                for k in range(6):
                    source = jnp.where(k < counts[box], lists[k, box] - base, 96)
                    total = total + rows_by_rows(held[source], blocks[box, k].reshape(128, 256))
                out[box] = total
            return carry

        lax.fori_loop(0, 2, body, 0, unroll=2)
        copies += begin(sems, (out.at[4 * t : 4 * t + 4], out_to.at[4 * t : 4 * t + 4]), first=13 + t)
    finish(*copies[13:])


def receive_kernel(l0, l1, l2, l3, x0, x1, x2, x3, near_from, out_to, codes, packs, samples, matrix, near, out, sems):
    copies = begin(
        sems,
        *[(l, codes.at[k]) for k, l in enumerate((l0, l1, l2, l3))],
        *[(x, packs.at[k]) for k, x in enumerate((x0, x1, x2, x3))],
        (near_from, near),
    )
    finish(*copies[0:4])
    for k in range(4):
        values = value_of(codes[k, 0:512]) * unit_of(codes[k, 512:528])
        samples[:, :, :, sender(k)] = values.reshape(4, 8, 2, 8, 128)
    finish(*copies[4:9])
    units = [unit_of(packs[k, 1024:1040]) for k in range(4)]

    def body(p, carry):
        for j in range(4):
            b = 4 * p + j
            rows = pl.ds(pl.multiple_of(32 * b, 32), 32)
            for k in range(4):
                matrix[b, sender(k)] = value_of(packs[k, rows, :]) * units[k]
            left_high, left_low = halves(samples[j, p].reshape(64, 128))
            high, low = halves(matrix[b].reshape(128, 128))
            left = jnp.concatenate([left_high, left_low], axis=1)
            right = jnp.concatenate(
                [jnp.concatenate([high, low], axis=1), jnp.concatenate([high, jnp.zeros_like(low)], axis=1)], axis=0
            )
            both = rows_by_cols(left, right)
            total = near[b] + (both[:, :128] + both[:, 128:])
            turned = swap_half(total)
            out[b, 0] = (total[:32] - turned[32:])[:, :64]
            out[b, 1] = (total[32:] + turned[:32])[:, :64]
        return carry

    for t in range(4):
        lax.fori_loop(2 * t, 2 * t + 2, body, 0, unroll=2)
        part = slice(8 * t, 8 * t + 8)
        copies += begin(sems, (out.at[part], out_to.at[part]), first=9 + t)
    finish(*copies[9:])


def around(x, axis, peers, k):
    return lax.ppermute(x, axis, [(i, (i + k) % peers) for i in range(peers)])


def after_all(values, *tokens):
    return lax.optimization_barrier((*values, *tokens))[: len(values)]


def shards(
    currents,
    near_blocks,
    near_list,
    near_count,
    radiate,
    receive,
    phase_one,
    phase_two,
    interp_one,
    interp_two,
    trans_one,
    kind_one,
    list_one,
    trans_two,
    kind_two,
    list_two,
):
    n_space = lax.axis_size("space")
    n_dir = lax.axis_size("dir")
    up = [(i, i + 1) for i in range(n_space - 1)]
    down = [(i + 1, i) for i in range(n_space - 1)]

    flat = currents.reshape(32, 64, 256)
    before = lax.ppermute(flat, "space", up)
    after = lax.ppermute(flat, "space", down)

    leaf = call(
        leaf_kernel,
        [((272, 128), I16)] * 4,
        [currents, radiate, trans_one, trans_two],
        [
            pltpu.VMEM((32, 2, 32, 256), BF16),
            pltpu.VMEM((32, 2, 32, 256), BF16),
            pltpu.VMEM((40, 2, 128), F32),
            pltpu.VMEM((40, 2, 512), F32),
            pltpu.VMEM((4, 128, 128), F32),
            pltpu.VMEM((4, 272, 128), I16),
        ],
        6,
        LARGE,
        "leaf",
        limit=62,
    )
    own_leaf = leaf[0]
    leaf = [own_leaf] + [around(leaf[k], "dir", n_dir, k) for k in (1, 2, 3)]
    angle_room = [*[pltpu.VMEM((4, 512), F32)] * 2, *[pltpu.VMEM((4, 2048), F32)] * 2]
    packed = call(
        pack_kernel,
        [((1040, 128), I16)] * 4 + [((4, 512), F32)] * 2 + [((4, 2048), F32)] * 2,
        list(after_all((receive, phase_one, phase_two), own_leaf)),
        [
            pltpu.VMEM((32, 2, 32, 256), F32),
            pltpu.VMEM((4, 512), F32),
            pltpu.VMEM((4, 2048), F32),
            *angle_room,
            pltpu.VMEM((4, 1040, 128), I16),
        ],
        8,
        SMALL,
        "pack",
    )
    packed, angles = packed[:4], packed[4:]
    leaf, packed, before, after = lax.optimization_barrier((leaf, packed, before, after))
    packed = [packed[0]] + [around(packed[k], "dir", n_dir, k) for k in (1, 2, 3)]


    parent, halo, message = call(
        lift_kernel,
        [((8, 2, 8, 512), F32), ((128, 512), BF16), ((32, 16, 128), F32)],
        leaf + [interp_one, interp_two] + list(angles),
        [
            pltpu.VMEM((512, 128), F32),
            pltpu.VMEM((2048, 512), F32),
            *angle_room,
            pltpu.VMEM((8, 2, 8, 512), F32),
            pltpu.VMEM((128, 512), BF16),
            pltpu.VMEM((32, 16, 128), F32),
            pltpu.VMEM((4, 272, 128), I16),
            pltpu.VMEM((4, 128, 128), F32),
            pltpu.VMEM((2, 4, 2, 8, 2048), F32),
        ],
        16,
        LARGE,
        "lift",
        landed=(1, 2, 3),
    )
    top = lax.all_to_all(message, "space", 0, 0)
    parents_before = lax.ppermute(halo, "space", up)
    parents_after = lax.ppermute(halo, "space", down)

    (moved,) = call(
        top_kernel,
        [((64, 8, 128), F32)],
        [kind_two.T, list_two.T, top.reshape(64, 8, 128)] + leaf,
        [
            pltpu.SMEM((8, 64), I32),
            pltpu.SMEM((8, 64), I32),
            pltpu.VMEM((64, 8, 128), F32),
            pltpu.VMEM((4, 144, 128), I16),
            pltpu.VMEM((40, 128), F32),
            pltpu.VMEM((40, 128), F32),
            pltpu.VMEM((64, 8, 128), F32),
        ],
        7,
        LARGE,
        "translate_two",
        landed=(2, 4, 5, 6),
    )
    arrived = lax.all_to_all(moved.reshape(32, 16, 128), "space", 0, 0)

    packed, parents_before, parents_after = lax.optimization_barrier((packed, parents_before, parents_after))
    (near_one,) = call(
        parent_kernel,
        [((8, 2, 8, 512), F32)],
        [kind_one, list_one, parents_before, parent, parents_after] + leaf,
        [
            pltpu.SMEM((8, 8), I32),
            pltpu.SMEM((8, 8), I32),
            pltpu.VMEM((128, 512), BF16),
            pltpu.VMEM((128, 512), BF16),
            pltpu.VMEM((24, 2, 8, 512), F32),
            pltpu.VMEM((4, 96, 128), I16),
            pltpu.VMEM((4, 80, 128), F32),
            pltpu.VMEM((8, 2, 8, 512), F32),
        ],
        9,
        SMALL,
        "translate_one",
        landed=(2, 4, 6, 7, 8),
    )

    (lowered,) = call(
        lower_kernel,
        [((528, 128), I16)],
        [arrived, near_one] + list(angles) + [interp_one, interp_two],
        [
            *angle_room,
            pltpu.VMEM((512, 128), F32),
            pltpu.VMEM((2048, 512), F32),
            pltpu.VMEM((32, 16, 128), F32),
            pltpu.VMEM((8, 2, 8, 512), F32),
            pltpu.VMEM((128, 2048), BF16),
            pltpu.VMEM((128, 2048), BF16),
            pltpu.VMEM((512, 128), F32),
            pltpu.VMEM((528, 128), I16),
        ],
        11,
        LARGE,
        "lower",
        landed=(0,),
    )
    shared = [around(lowered, "dir", n_dir, k) for k in (1, 2, 3)]

    (near,) = call(
        near_kernel,
        [((32, 64, 128), F32)],
        [near_list.T, near_count, before, flat, after, near_blocks],
        [
            pltpu.SMEM((6, 32), I32),
            pltpu.SMEM((32,), I32),
            pltpu.VMEM((97, 64, 256), BF16),
            pltpu.VMEM((32, 6, 2, 64, 256), BF16),
            pltpu.VMEM((32, 64, 128), F32),
        ],
        21,
        SMALL,
        "near",
        limit=62,
        landed=(2, 4),
    )
    (fields,) = call(
        receive_kernel,
        [((32, 2, 32, 64), F32)],
        [lowered] + shared + packed + [near],
        [
            pltpu.VMEM((4, 528, 128), I16),
            pltpu.VMEM((4, 1040, 128), I16),
            pltpu.VMEM((4, 8, 2, 4, 8, 128), F32),
            pltpu.VMEM((32, 4, 32, 128), F32),
            pltpu.VMEM((32, 64, 128), F32),
            pltpu.VMEM((32, 2, 32, 64), F32),
        ],
        13,
        LARGE,
        "receive",
        landed=(1, 2, 3, 5, 6, 7),
    )
    return fields


def solution(mesh):
    in_specs = (
        P("space", None, None, None),
        P("space", None, None, "dir", None),
        P("space", None),
        P("space"),
        P("space", None, "dir", None),
        P("space", None, "dir", None),
        P(),
        P(),
        P(),
        P(),
        P(None, None, "dir"),
        P("space", None),
        P("space", None),
        P(None, None, "dir"),
        P(),
        P(),
    )
    out_specs = P("space", None, None, "dir")
    return jax.shard_map(shards, mesh=mesh, in_specs=in_specs, out_specs=out_specs, check_vma=False)
```

profile of v0, /device:TPU:1, one launch (start us, length us, event | category | flops | bytes accessed | tf_op | source)
XLA Modules:
  0.0 85.1 jit_solution(12426406288767585561)
XLA Ops:
  0.0 4.7 %collective-permute-start.3 = (bf16[32,64,256]{2,1,0:T(8,128)(2,1)}, bf16[32,64,256]{2,1,0:T(8,128)(2,1)}, u32[]{:S(2)}, u32[]{:S(2)}) collective-permute-start(bf16[32,64,256]{2,1,0:T(8,128)(2,1)} %bitcast.9), channel_id=1, source_target_pairs={{0,4},{4,8},{8,12},{12,16},{16,20},{20,24},{24,28},{28,32},{32,36}... | collective-permute-start | bytes 3145736 | tf_op jit(solution)/shard_map/ppermute | solution.py:507
  4.7 1.9 %collective-permute-start.4 = (bf16[32,64,256]{2,1,0:T(8,128)(2,1)}, bf16[32,64,256]{2,1,0:T(8,128)(2,1)}, u32[]{:S(2)}, u32[]{:S(2)}) collective-permute-start(bf16[32,64,256]{2,1,0:T(8,128)(2,1)} %bitcast.10), channel_id=1, source_target_pairs={{4,0},{8,4},{12,8},{16,12},{20,16},{24,20},{28,24},{32,28},{36,32}... | collective-permute-start | bytes 3145736 | tf_op jit(solution)/shard_map/ppermute | solution.py:508
  6.7 3.1 %leaf.1 = (s16[272,128]{1,0:T(8,128)(2,1)}, s16[272,128]{1,0:T(8,128)(2,1)}, s16[272,128]{1,0:T(8,128)(2,1)}, s16[272,128]{1,0:T(8,128)(2,1)}) custom-call(bf16[32,2,32,256]{3,2,1,0:T(8,128)(2,1)} %cur_from.1, bf16[32,2,32,256]{3,2,1,0:T(8,128)(2,1)} %rad_from.1, f32[40,2,128]{2,1,0:T(2,128)} %one_from.1, f32[40,2,512]{2,1,0:T(2,128)} %two_from.1), custom_call_target="tpu_custom_call" | custom-call | flops 68719476736 | bytes 68719476736 | tf_op jit(solution)/shard_map/leaf/pallas_call | solution.py:21
  9.8 1.7 %collective-permute-start = (s16[272,128]{1,0:T(8,128)(2,1)}, s16[272,128]{1,0:T(8,128)(2,1)S(1)}, u32[]{:S(2)}, u32[]{:S(2)}) collective-permute-start(s16[272,128]{1,0:T(8,128)(2,1)} %get-tuple-element.40), channel_id=1, source_target_pairs={{0,1},{1,2},{2,3},{3,0},{4,5},{5,6},{6,7},{7,4},{8,9},{9,10},{10,1... | collective-permute-start | bytes 208904 | tf_op jit(solution)/shard_map/ppermute | solution.py:476
  11.5 3.3 %collective-permute-start.1 = (s16[272,128]{1,0:T(8,128)(2,1)}, s16[272,128]{1,0:T(8,128)(2,1)S(1)}, u32[]{:S(2)}, u32[]{:S(2)}) collective-permute-start(s16[272,128]{1,0:T(8,128)(2,1)} %get-tuple-element.41), channel_id=1, source_target_pairs={{0,2},{1,3},{2,0},{3,1},{4,6},{5,7},{6,4},{7,5},{8,10},{9,11},{10,... | collective-permute-start | bytes 208904 | tf_op jit(solution)/shard_map/ppermute | solution.py:476
  15.5 3.1 %pack.1 = (s16[1040,128]{1,0:T(8,128)(2,1)S(1)}, s16[1040,128]{1,0:T(8,128)(2,1)S(1)}, s16[1040,128]{1,0:T(8,128)(2,1)S(1)}, s16[1040,128]{1,0:T(8,128)(2,1)S(1)...) custom-call(f32[32,2,32,256]{3,2,1,0:T(8,128)} %rec_from, ...), custom_call_target="tpu_custom_call" | custom-call | flops 4096 | bytes 4096 | tf_op jit(solution)/shard_map/pack/pallas_call | solution.py:21
  19.2 2.0 %collective-permute-done.4.after = bf16[32,64,256]{2,1,0:T(8,128)(2,1)} collective-permute-done((bf16[32,64,256]{2,1,0:T(8,128)(2,1)}, bf16[32,64,256]{2,1,0:T(8,128)(2,1)}, u32[]{:S(2)}, u32[]{:S(2)}) %collective-permute-start.4) | collective-permute-done | bytes 1048608 | tf_op jit(solution)/shard_map/ppermute | solution.py:508
  21.2 0.9 %copy-done = s16[272,128]{1,0:T(8,128)(2,1)S(1)} copy-done((s16[272,128]{1,0:T(8,128)(2,1)S(1)}, s16[272,128]{1,0:T(8,128)(2,1)}, u32[]{:S(2)}) %copy-start) | copy-done | bytes 69656
  22.1 5.2 %lift.1 = (f32[8,2,8,512]{3,2,1,0:T(8,128)S(1)}, bf16[128,512]{1,0:T(8,128)(2,1)S(1)}, f32[32,16,128]{2,1,0:T(8,128)}) custom-call(s16[272,128]{1,0:T(8,128)(2,1)S(1)} %copy-done, s16[272,128]{1,0:T(8,128)(2,1)S(1)} %collective-permute-done.r1.m1, s16[272,128]{1,0:T(8,128)(2,1)S(1)} %collective-permute-done.1.r2.m2, ...), custom_call_target="tpu_custom_call" | custom-call | flops 68719476736 | bytes 68719476736 | tf_op jit(solution)/shard_map/lift/pallas_call | solution.py:21
  27.3 8.4 %all-to-all-start = ((f32[32,16,128]{2,1,0:T(8,128)}), f32[32,16,128]{2,1,0:T(8,128)S(1)}, u32[]{:S(2)}, u32[]{:S(2)}) async-start(f32[32,16,128]{2,1,0:T(8,128)} %get-tuple-element.58), calls=%async_computation | async-start | bytes 524288 | tf_op jit(solution)/shard_map/all_to_all | solution.py:570
  35.8 1.7 %collective-permute-start.5 = (s16[1040,128]{1,0:T(8,128)(2,1)S(1)}, s16[1040,128]{1,0:T(8,128)(2,1)S(1)}, u32[]{:S(2)}, u32[]{:S(2)}) collective-permute-start(s16[1040,128]{1,0:T(8,128)(2,1)S(1)} %get-tuple-element.60), channel_id=1, source_target_pairs={{0,1},{1,2},{2,3},{3,0},{4,5},{5,6},{6,7},{7,4},{8,9},{9,10},{10,1... | collective-permute-start | bytes 798728 | tf_op jit(solution)/shard_map/ppermute | solution.py:476
  37.5 3.3 %collective-permute-start.6 = (s16[1040,128]{1,0:T(8,128)(2,1)S(1)}, s16[1040,128]{1,0:T(8,128)(2,1)S(1)}, u32[]{:S(2)}, u32[]{:S(2)}) collective-permute-start(s16[1040,128]{1,0:T(8,128)(2,1)S(1)} %get-tuple-element.61), channel_id=1, source_target_pairs={{0,2},{1,3},{2,0},{3,1},{4,6},{5,7},{6,4},{7,5},{8,10},{9,11},{10,... | collective-permute-start | bytes 798728 | tf_op jit(solution)/shard_map/ppermute | solution.py:476
  41.5 3.3 %all-to-all-done = f32[32,16,128]{2,1,0:T(8,128)S(1)} async-done(((f32[32,16,128]{2,1,0:T(8,128)}), f32[32,16,128]{2,1,0:T(8,128)S(1)}, u32[]{:S(2)}, u32[]{:S(2)}) %all-to-all-start) | async-done | bytes 262176 | tf_op jit(solution)/shard_map/all_to_all | solution.py:570
  44.8 3.4 %translate_two.1 = f32[64,8,128]{2,1,0:T(8,128)} custom-call(s32[8,64]{1,0:T(8,128)S(1)} %bitcast.7, s32[8,64]{1,0:T(8,128)S(1)} %bitcast.8, f32[64,8,128]{2,1,0:T(8,128)S(1)} %bitcast.6, s16[272,128]{1,0:T(8,128)(2,1)S(1)} %copy-done.1, s16[272,128]{1,0:T(8,128)(2,1)S(1)} %collective-permute-done.r1.m1, s16[272,128]{1,0:T(8,128)(2,1)S(1)} %collective-permute-done.1.r2.m2, ...), custom_call_target="tpu_custom_call" | custom-call | flops 68719476736 | bytes 68719476736 | tf_op jit(solution)/shard_map/translate_two/pallas_call | solution.py:21
  48.2 5.0 %all-to-all-start.1 = ((f32[32,16,128]{2,1,0:T(8,128)}), f32[32,16,128]{2,1,0:T(8,128)S(1)}, u32[]{:S(2)}, u32[]{:S(2)}) async-start(f32[32,16,128]{2,1,0:T(8,128)} %bitcast.4), calls=%async_computation.1 | async-start | bytes 524288 | tf_op jit(solution)/shard_map/all_to_all | solution.py:592
  53.2 3.5 %collective-permute-start.8 = (bf16[128,512]{1,0:T(8,128)(2,1)S(1)}, bf16[128,512]{1,0:T(8,128)(2,1)S(1)}, u32[]{:S(2)}, u32[]{:S(2)}) collective-permute-start(bf16[128,512]{1,0:T(8,128)(2,1)S(1)} %get-tuple-element.63), channel_id=1, source_target_pairs={{0,4},{4,8},{8,12},{12,16},{16,20},{20,24},{24,28},{28,32},{32,36}... | collective-permute-start | bytes 393224 | tf_op jit(solution)/shard_map/ppermute | solution.py:571
  56.7 1.9 %collective-permute-start.9 = (bf16[128,512]{1,0:T(8,128)(2,1)S(1)}, bf16[128,512]{1,0:T(8,128)(2,1)S(1)}, u32[]{:S(2)}, u32[]{:S(2)}) collective-permute-start(bf16[128,512]{1,0:T(8,128)(2,1)S(1)} %get-tuple-element.63), channel_id=1, source_target_pairs={{4,0},{8,4},{12,8},{16,12},{20,16},{24,20},{28,24},{32,28},{36,32}... | collective-permute-start | bytes 393224 | tf_op jit(solution)/shard_map/ppermute | solution.py:572
  59.4 3.6 %collective-permute-done.9.after_from = bf16[128,512]{1,0:T(8,128)(2,1)S(1)} collective-permute-done((bf16[128,512]{1,0:T(8,128)(2,1)S(1)}, bf16[128,512]{1,0:T(8,128)(2,1)S(1)}, u32[]{:S(2)}, u32[]{:S(2)}) %collective-permute-start.9) | collective-permute-done | bytes 131104 | tf_op jit(solution)/shard_map/ppermute | solution.py:572
  63.0 1.2 %translate_one.1.near_one_from = f32[8,2,8,512]{3,2,1,0:T(8,128)S(1)} custom-call(s32[8,8]{1,0:T(8,128)S(1)} %copy-done.4, s32[8,8]{1,0:T(8,128)S(1)} %copy-done.5, bf16[128,512]{1,0:T(8,128)(2,1)S(1)} %collective-permute-done.8.before_from, f32[8,2,8,512]{3,2,1,0:T(8,128)S(1)} %get-tuple-element.65.parent_from, ...), custom_call_target="tpu_custom_call" | custom-call | flops 4096 | bytes 4096 | tf_op jit(solution)/shard_map/translate_one/pallas_call | solution.py:21
  64.2 3.8 %lower.1.l0 = s16[528,128]{1,0:T(8,128)(2,1)S(1)} custom-call(f32[32,16,128]{2,1,0:T(8,128)S(1)} %all-to-all-done.1.arrived_from, f32[8,2,8,512]{3,2,1,0:T(8,128)S(1)} %translate_one.1.near_one_from, f32[4,512]{1,0:T(4,128)S(1)} %get-tuple-element.54.refs_2_.refs_0_, f32[4,512]{1,0:T(4,128)S(1)} %get-tuple-element.55.refs_3_.refs_1_, ...), custom_call_target="tpu_custom_call" | custom-call | flops 68719476736 | bytes 68719476736 | tf_op jit(solution)/shard_map/lower/pallas_call | solution.py:21
  68.1 0.8 collective-permute-start.10
  68.9 2.9 %collective-permute-start.11 = (s16[528,128]{1,0:T(8,128)(2,1)S(1)}, s16[528,128]{1,0:T(8,128)(2,1)S(1)}, u32[]{:S(2)}, u32[]{:S(2)}) collective-permute-start(s16[528,128]{1,0:T(8,128)(2,1)S(1)} %lower.1.l0), channel_id=1, source_target_pairs={{0,2},{1,3},{2,0},{3,1},{4,6},{5,7},{6,4},{7,5},{8,10},{9,11},{10,... | collective-permute-start | bytes 405512 | tf_op jit(solution)/shard_map/ppermute | solution.py:476
  72.5 8.4 %near.1.near_from = f32[32,64,128]{2,1,0:T(8,128)} custom-call(s32[6,32]{1,0:T(8,128)} %bitcast.12, s32[32]{0:T(128)} %counts_from.1, bf16[32,64,256]{2,1,0:T(8,128)(2,1)} %collective-permute-done.3.before, bf16[32,64,256]{2,1,0:T(8,128)(2,1)} %bitcast.11, bf16[32,64,256]{2,1,0:T(8,128)(2,1)} %collective-permute-done.4.after, ...), custom_call_target="tpu_custom_call" | custom-call | flops 4096 | bytes 4096 | tf_op jit(solution)/shard_map/near/pallas_call | solution.py:21
  81.0 4.0 %receive.1 = f32[32,2,32,64]{3,2,1,0:T(8,128)} custom-call(s16[528,128]{1,0:T(8,128)(2,1)S(1)} %lower.1.l0, s16[528,128]{1,0:T(8,128)(2,1)S(1)} %collective-permute-done.10.l1, s16[528,128]{1,0:T(8,128)(2,1)S(1)} %collective-permute-done.11.l2, s16[528,128]{1,0:T(8,128)(2,1)S(1)} %collective-permute-done.12.l3, s16[1040,128]{1,0:T(8,128)(2,1)S(1)} %get-tuple-element.67.x0, ...), custom_call_target="tpu_custom_call" | custom-call | flops 68719476736 | bytes 68719476736 | tf_op jit(solution)/shard_map/receive/pallas_call | solution.py:21
  (32 shorter events, 3.5 us)
Async XLA Ops:
  0.0 15.5 %copy-start.2 = (f32[4,2048]{1,0:T(4,128)S(1)}, f32[4,2048]{1,0:T(4,128)}, u32[]{:S(2)}) copy-start(f32[4,2048]{1,0:T(4,128)} %two_from.2) | copy-start | bytes 98308
  0.0 15.5 %copy-start.3 = (f32[4,512]{1,0:T(4,128)S(1)}, f32[4,512]{1,0:T(4,128)}, u32[]{:S(2)}) copy-start(f32[4,512]{1,0:T(4,128)} %one_from.2) | copy-start | bytes 24580
  0.0 21.2 %copy-start.6 = (f32[512,128]{1,0:T(8,128)S(1)}, f32[512,128]{1,0:T(8,128)}, u32[]{:S(2)}) copy-start(f32[512,128]{1,0:T(8,128)} %refs_4_.1) | copy-start | bytes 786436
  0.0 19.2 %collective-permute-start.3 = (bf16[32,64,256]{2,1,0:T(8,128)(2,1)}, bf16[32,64,256]{2,1,0:T(8,128)(2,1)}, u32[]{:S(2)}, u32[]{:S(2)}) collective-permute-start(bf16[32,64,256]{2,1,0:T(8,128)(2,1)} %bitcast.9), channel_id=1, source_target_pairs={{0,4},{4,8},{8,12},{12,16},{16,20},{20,24},{24,28},{28,32},{32,36}... | collective-permute-start | bytes 3145736 | tf_op jit(solution)/shard_map/ppermute | solution.py:507
  4.7 16.4 %collective-permute-start.4 = (bf16[32,64,256]{2,1,0:T(8,128)(2,1)}, bf16[32,64,256]{2,1,0:T(8,128)(2,1)}, u32[]{:S(2)}, u32[]{:S(2)}) collective-permute-start(bf16[32,64,256]{2,1,0:T(8,128)(2,1)} %bitcast.10), channel_id=1, source_target_pairs={{4,0},{8,4},{12,8},{16,12},{20,16},{24,20},{28,24},{32,28},{36,32}... | collective-permute-start | bytes 3145736 | tf_op jit(solution)/shard_map/ppermute | solution.py:508
  9.8 8.8 %collective-permute-start = (s16[272,128]{1,0:T(8,128)(2,1)}, s16[272,128]{1,0:T(8,128)(2,1)S(1)}, u32[]{:S(2)}, u32[]{:S(2)}) collective-permute-start(s16[272,128]{1,0:T(8,128)(2,1)} %get-tuple-element.40), channel_id=1, source_target_pairs={{0,1},{1,2},{2,3},{3,0},{4,5},{5,6},{6,7},{7,4},{8,9},{9,10},{10,1... | collective-permute-start | bytes 208904 | tf_op jit(solution)/shard_map/ppermute | solution.py:476
  11.5 7.1 %collective-permute-start.1 = (s16[272,128]{1,0:T(8,128)(2,1)}, s16[272,128]{1,0:T(8,128)(2,1)S(1)}, u32[]{:S(2)}, u32[]{:S(2)}) collective-permute-start(s16[272,128]{1,0:T(8,128)(2,1)} %get-tuple-element.41), channel_id=1, source_target_pairs={{0,2},{1,3},{2,0},{3,1},{4,6},{5,7},{6,4},{7,5},{8,10},{9,11},{10,... | collective-permute-start | bytes 208904 | tf_op jit(solution)/shard_map/ppermute | solution.py:476
  14.8 4.4 %collective-permute-start.2 = (s16[272,128]{1,0:T(8,128)(2,1)}, s16[272,128]{1,0:T(8,128)(2,1)S(1)}, u32[]{:S(2)}, u32[]{:S(2)}) collective-permute-start(s16[272,128]{1,0:T(8,128)(2,1)} %get-tuple-element.42), channel_id=1, source_target_pairs={{0,3},{1,0},{2,1},{3,2},{4,7},{5,4},{6,5},{7,6},{8,11},{9,8},{10,9... | collective-permute-start | bytes 208904 | tf_op jit(solution)/shard_map/ppermute | solution.py:476
  21.2 0.9 %copy-start = (s16[272,128]{1,0:T(8,128)(2,1)S(1)}, s16[272,128]{1,0:T(8,128)(2,1)}, u32[]{:S(2)}) copy-start(s16[272,128]{1,0:T(8,128)(2,1)} %get-tuple-element.50.r0.m0) | copy-start | bytes 208900
  22.1 22.7 %copy-start.1 = (s16[272,128]{1,0:T(8,128)(2,1)S(1)}, s16[272,128]{1,0:T(8,128)(2,1)}, u32[]{:S(2)}) copy-start(s16[272,128]{1,0:T(8,128)(2,1)} %get-tuple-element.50.r0.m0) | copy-start | bytes 208900
  22.1 22.7 %copy-start.7 = (s32[64,8]{0,1:T(8,128)S(1)}, s32[64,8]{0,1:T(8,128)}, u32[]{:S(2)}) copy-start(s32[64,8]{0,1:T(8,128)} %param.30) | copy-start | bytes 6148
  22.1 22.7 %copy-start.8 = (s32[64,8]{0,1:T(8,128)S(1)}, s32[64,8]{0,1:T(8,128)}, u32[]{:S(2)}) copy-start(s32[64,8]{0,1:T(8,128)} %param.31) | copy-start | bytes 6148
  27.3 17.4 %all-to-all-start = ((f32[32,16,128]{2,1,0:T(8,128)}), f32[32,16,128]{2,1,0:T(8,128)S(1)}, u32[]{:S(2)}, u32[]{:S(2)}) async-start(f32[32,16,128]{2,1,0:T(8,128)} %get-tuple-element.58), calls=%async_computation | async-start | bytes 524288 | tf_op jit(solution)/shard_map/all_to_all | solution.py:570
  35.8 27.2 %collective-permute-start.5 = (s16[1040,128]{1,0:T(8,128)(2,1)S(1)}, s16[1040,128]{1,0:T(8,128)(2,1)S(1)}, u32[]{:S(2)}, u32[]{:S(2)}) collective-permute-start(s16[1040,128]{1,0:T(8,128)(2,1)S(1)} %get-tuple-element.60), channel_id=1, source_target_pairs={{0,1},{1,2},{2,3},{3,0},{4,5},{5,6},{6,7},{7,4},{8,9},{9,10},{10,1... | collective-permute-start | bytes 798728 | tf_op jit(solution)/shard_map/ppermute | solution.py:476
  37.5 25.5 %collective-permute-start.6 = (s16[1040,128]{1,0:T(8,128)(2,1)S(1)}, s16[1040,128]{1,0:T(8,128)(2,1)S(1)}, u32[]{:S(2)}, u32[]{:S(2)}) collective-permute-start(s16[1040,128]{1,0:T(8,128)(2,1)S(1)} %get-tuple-element.61), channel_id=1, source_target_pairs={{0,2},{1,3},{2,0},{3,1},{4,6},{5,7},{6,4},{7,5},{8,10},{9,11},{10,... | collective-permute-start | bytes 798728 | tf_op jit(solution)/shard_map/ppermute | solution.py:476
  40.8 22.2 %collective-permute-start.7 = (s16[1040,128]{1,0:T(8,128)(2,1)S(1)}, s16[1040,128]{1,0:T(8,128)(2,1)S(1)}, u32[]{:S(2)}, u32[]{:S(2)}) collective-permute-start(s16[1040,128]{1,0:T(8,128)(2,1)S(1)} %get-tuple-element.62), channel_id=1, source_target_pairs={{0,3},{1,0},{2,1},{3,2},{4,7},{5,4},{6,5},{7,6},{8,11},{9,8},{10,9... | collective-permute-start | bytes 798728 | tf_op jit(solution)/shard_map/ppermute | solution.py:476
  44.8 18.2 %copy-start.4 = (s32[8,8]{1,0:T(8,128)S(1)}, s32[8,8]{1,0:T(8,128)}, u32[]{:S(2)}) copy-start(s32[8,8]{1,0:T(8,128)} %kinds_from.1) | copy-start | bytes 772
  44.8 18.2 %copy-start.5 = (s32[8,8]{1,0:T(8,128)S(1)}, s32[8,8]{1,0:T(8,128)}, u32[]{:S(2)}) copy-start(s32[8,8]{1,0:T(8,128)} %lists_from.1) | copy-start | bytes 772
  48.2 16.1 %all-to-all-start.1 = ((f32[32,16,128]{2,1,0:T(8,128)}), f32[32,16,128]{2,1,0:T(8,128)S(1)}, u32[]{:S(2)}, u32[]{:S(2)}) async-start(f32[32,16,128]{2,1,0:T(8,128)} %bitcast.4), calls=%async_computation.1 | async-start | bytes 524288 | tf_op jit(solution)/shard_map/all_to_all | solution.py:592
  53.2 6.2 %collective-permute-start.8 = (bf16[128,512]{1,0:T(8,128)(2,1)S(1)}, bf16[128,512]{1,0:T(8,128)(2,1)S(1)}, u32[]{:S(2)}, u32[]{:S(2)}) collective-permute-start(bf16[128,512]{1,0:T(8,128)(2,1)S(1)} %get-tuple-element.63), channel_id=1, source_target_pairs={{0,4},{4,8},{8,12},{12,16},{16,20},{20,24},{24,28},{28,32},{32,36}... | collective-permute-start | bytes 393224 | tf_op jit(solution)/shard_map/ppermute | solution.py:571
  56.7 6.3 %collective-permute-start.9 = (bf16[128,512]{1,0:T(8,128)(2,1)S(1)}, bf16[128,512]{1,0:T(8,128)(2,1)S(1)}, u32[]{:S(2)}, u32[]{:S(2)}) collective-permute-start(bf16[128,512]{1,0:T(8,128)(2,1)S(1)} %get-tuple-element.63), channel_id=1, source_target_pairs={{4,0},{8,4},{12,8},{16,12},{20,16},{24,20},{28,24},{32,28},{36,32}... | collective-permute-start | bytes 393224 | tf_op jit(solution)/shard_map/ppermute | solution.py:572
  68.1 12.9 %collective-permute-start.10 = (s16[528,128]{1,0:T(8,128)(2,1)S(1)}, s16[528,128]{1,0:T(8,128)(2,1)S(1)}, u32[]{:S(2)}, u32[]{:S(2)}) collective-permute-start(s16[528,128]{1,0:T(8,128)(2,1)S(1)} %lower.1.l0), channel_id=1, source_target_pairs={{0,1},{1,2},{2,3},{3,0},{4,5},{5,6},{6,7},{7,4},{8,9},{9,10},{10,1... | collective-permute-start | bytes 405512 | tf_op jit(solution)/shard_map/ppermute | solution.py:476
  68.9 12.1 %collective-permute-start.11 = (s16[528,128]{1,0:T(8,128)(2,1)S(1)}, s16[528,128]{1,0:T(8,128)(2,1)S(1)}, u32[]{:S(2)}, u32[]{:S(2)}) collective-permute-start(s16[528,128]{1,0:T(8,128)(2,1)S(1)} %lower.1.l0), channel_id=1, source_target_pairs={{0,2},{1,3},{2,0},{3,1},{4,6},{5,7},{6,4},{7,5},{8,10},{9,11},{10,... | collective-permute-start | bytes 405512 | tf_op jit(solution)/shard_map/ppermute | solution.py:476
  71.8 9.2 %collective-permute-start.12 = (s16[528,128]{1,0:T(8,128)(2,1)S(1)}, s16[528,128]{1,0:T(8,128)(2,1)S(1)}, u32[]{:S(2)}, u32[]{:S(2)}) collective-permute-start(s16[528,128]{1,0:T(8,128)(2,1)S(1)} %lower.1.l0), channel_id=1, source_target_pairs={{0,3},{1,0},{2,1},{3,2},{4,7},{5,4},{6,5},{7,6},{8,11},{9,8},{10,9... | collective-permute-start | bytes 405512 | tf_op jit(solution)/shard_map/ppermute | solution.py:476
where the time goes:
time: 86.6 us; the launch traced here: 85.1 us
  starting transfers between devices  41.5 us (48%)
  Pallas kernels  32.2 us (37%)
  waiting for transfers between devices  10.2 us (12%)
  local copies, waits for them, and re-layouts  0.92 us (1%)
    pallas_call x8, Pallas kernels, call(): pl.pallas_call(kernel, out_shape=shapes, in_specs=[ANYWHERE if n in lande...  32.2 us
    ppermute x9, starting transfers between devices, around(): return lax.ppermute(x, axis, [(i, (i + k) % peers) for i in range(peers)])  15.9 us
    all_to_all x1, starting transfers between devices, shards(): top = lax.all_to_all(message, 'space', 0, 0)  8.43 us
    all_to_all x1, starting transfers between devices, shards(): arrived = lax.all_to_all(moved.reshape(32, 16, 128), 'space', 0, 0)  4.99 us
    ppermute x1, starting transfers between devices, shards(): before = lax.ppermute(flat, 'space', up)  4.73 us
    ppermute x1, waiting for transfers between devices, shards(): parents_after = lax.ppermute(halo, 'space', down)  3.6 us
    ppermute x1, starting transfers between devices, shards(): parents_before = lax.ppermute(halo, 'space', up)  3.54 us
    all_to_all x1, waiting for transfers between devices, shards(): top = lax.all_to_all(message, 'space', 0, 0)  3.26 us
  transfers between devices with their start and end apart: 15, of which 5 were waited for; matrix products, arithmetic and copies ran while one was open for 0% of the time, Pallas kernels for 23%

commit v1 on v0

--- a/solution.py
+++ b/solution.py
@@ -1,3 +1,5 @@
+import functools
+
 import jax
 import jax.numpy as jnp
 from jax import lax
@@ -10,19 +12,20 @@
 I32 = jnp.int32
 I16 = jnp.int16
 IN_HBM = pl.BlockSpec(memory_space=pltpu.HBM)
+IN_VMEM = pl.BlockSpec(memory_space=pltpu.VMEM)
 ANYWHERE = pl.BlockSpec(memory_space=pl.ANY)
 MIB = 1024 * 1024
 SMALL = 2**12
 LARGE = 2**36
 
 
-def call(kernel, outs, operands, scratch, copies, cost, name, landed=(), limit=52):
+def call(kernel, outs, operands, scratch, copies, cost, name, landed=(), limit=52, kept=()):
     shapes = tuple(jax.ShapeDtypeStruct(shape, kind) for shape, kind in outs)
     return pl.pallas_call(
         kernel,
         out_shape=shapes,
         in_specs=[ANYWHERE if n in landed else IN_HBM for n in range(len(operands))],
-        out_specs=tuple(IN_HBM for _ in outs),
+        out_specs=tuple(IN_VMEM if n in kept else IN_HBM for n in range(len(outs))),
         scratch_shapes=[*scratch, pltpu.SemaphoreType.DMA((copies,))],
         compiler_params=pltpu.CompilerParams(vmem_limit_bytes=limit * MIB),
         cost_estimate=pl.CostEstimate(flops=cost, bytes_accessed=cost, transcendentals=0),
@@ -401,49 +404,57 @@
     finish(*begin(sems, (out, out_to)))
 
 
-def near_kernel(lists_from, counts_from, before, current, after, blocks_from, out_to, lists, counts, held, blocks, out, sems):
+def near_kernel(half, lists_from, counts_from, before, current, after, blocks_from, out_to, lists, counts, held, blocks, out, sems):
+    if half == 0:
+        sources = [(before, held.at[0:32]), (after.at[0:16], held.at[64:80])]
+    else:
+        sources = [(before.at[16:32], held.at[16:32]), (after, held.at[64:96])]
     copies = begin(
         sems,
         (lists_from, lists),
         (counts_from, counts),
-        (before, held.at[0:32]),
         (current, held.at[32:64]),
-        (after, held.at[64:96]),
-        *[(blocks_from.at[4 * t : 4 * t + 4], blocks.at[4 * t : 4 * t + 4]) for t in range(8)],
+        *sources,
+        *[
+            (blocks_from.at[16 * half + 4 * t : 16 * half + 4 * t + 4], blocks.at[4 * t : 4 * t + 4])
+            for t in range(4)
+        ],
     )
     held[96] = jnp.zeros((64, 256), BF16)
     finish(*copies[0:5])
     base = lax.axis_index("space") * 32 - 32
 
-    for t in range(8):
+    for t in range(4):
         finish(copies[5 + t])
 
         def body(n, carry):
-            for box in (4 * t + 2 * n, 4 * t + 2 * n + 1):
+            for row in (4 * t + 2 * n, 4 * t + 2 * n + 1):
+                box = 16 * half + row
                 total = jnp.zeros((64, 128), F32)
                 for k in range(6):
                     source = jnp.where(k < counts[box], lists[k, box] - base, 96)
-                    total = total + rows_by_rows(held[source], blocks[box, k].reshape(128, 256))
-                out[box] = total
+                    total = total + rows_by_rows(held[source], blocks[row, k].reshape(128, 256))
+                out[row] = total
             return carry
 
         lax.fori_loop(0, 2, body, 0, unroll=2)
-        copies += begin(sems, (out.at[4 * t : 4 * t + 4], out_to.at[4 * t : 4 * t + 4]), first=13 + t)
-    finish(*copies[13:])
-
-
-def receive_kernel(l0, l1, l2, l3, x0, x1, x2, x3, near_from, out_to, codes, packs, samples, matrix, near, out, sems):
+        copies += begin(sems, (out.at[4 * t : 4 * t + 4], out_to.at[4 * t : 4 * t + 4]), first=9 + t)
+    finish(*copies[9:])
+
+
+def receive_kernel(l0, l1, l2, l3, x0, x1, x2, x3, near_first, near_second, out_to, codes, packs, samples, matrix, near, out, sems):
     copies = begin(
         sems,
         *[(l, codes.at[k]) for k, l in enumerate((l0, l1, l2, l3))],
         *[(x, packs.at[k]) for k, x in enumerate((x0, x1, x2, x3))],
-        (near_from, near),
+        (near_first, near.at[0:16]),
+        (near_second, near.at[16:32]),
     )
     finish(*copies[0:4])
     for k in range(4):
         values = value_of(codes[k, 0:512]) * unit_of(codes[k, 512:528])
         samples[:, :, :, sender(k)] = values.reshape(4, 8, 2, 8, 128)
-    finish(*copies[4:9])
+    finish(*copies[4:10])
     units = [unit_of(packs[k, 1024:1040]) for k in range(4)]
 
     def body(p, carry):
@@ -468,8 +479,28 @@
     for t in range(4):
         lax.fori_loop(2 * t, 2 * t + 2, body, 0, unroll=2)
         part = slice(8 * t, 8 * t + 8)
-        copies += begin(sems, (out.at[part], out_to.at[part]), first=9 + t)
-    finish(*copies[9:])
+        copies += begin(sems, (out.at[part], out_to.at[part]), first=10 + t)
+    finish(*copies[10:])
+
+
+def near_half(half, *operands):
+    return call(
+        functools.partial(near_kernel, half),
+        [((16, 64, 128), F32)],
+        list(operands),
+        [
+            pltpu.SMEM((6, 32), I32),
+            pltpu.SMEM((32,), I32),
+            pltpu.VMEM((97, 64, 256), BF16),
+            pltpu.VMEM((16, 6, 2, 64, 256), BF16),
+            pltpu.VMEM((16, 64, 128), F32),
+        ],
+        13,
+        SMALL,
+        "near",
+        limit=60,
+        landed=(2, 4),
+    )[0]
 
 
 def around(x, axis, peers, k):
@@ -522,7 +553,8 @@
         6,
         LARGE,
         "leaf",
-        limit=62,
+        limit=60,
+        kept=(0,),
     )
     own_leaf = leaf[0]
     leaf = [own_leaf] + [around(leaf[k], "dir", n_dir, k) for k in (1, 2, 3)]
@@ -565,12 +597,13 @@
         16,
         LARGE,
         "lift",
-        landed=(1, 2, 3),
+        landed=(0, 1, 2, 3),
     )
     top = lax.all_to_all(message, "space", 0, 0)
     parents_before = lax.ppermute(halo, "space", up)
     parents_after = lax.ppermute(halo, "space", down)
 
+    top, parents_before, parents_after = lax.optimization_barrier((top, parents_before, parents_after))
     (moved,) = call(
         top_kernel,
         [((64, 8, 128), F32)],
@@ -587,11 +620,11 @@
         7,
         LARGE,
         "translate_two",
-        landed=(2, 4, 5, 6),
+        landed=(2, 3, 4, 5, 6),
     )
     arrived = lax.all_to_all(moved.reshape(32, 16, 128), "space", 0, 0)
 
-    packed, parents_before, parents_after = lax.optimization_barrier((packed, parents_before, parents_after))
+    near_parts = [near_half(half, near_list.T, near_count, before, flat, after, near_blocks) for half in (0, 1)]
     (near_one,) = call(
         parent_kernel,
         [((8, 2, 8, 512), F32)],
@@ -609,9 +642,10 @@
         9,
         SMALL,
         "translate_one",
-        landed=(2, 4, 6, 7, 8),
-    )
-
+        landed=(2, 4, 5, 6, 7, 8),
+    )
+
+    arrived, near_one, near_parts[0] = lax.optimization_barrier((arrived, near_one, near_parts[0]))
     (lowered,) = call(
         lower_kernel,
         [((528, 128), I16)],
@@ -634,27 +668,10 @@
     )
     shared = [around(lowered, "dir", n_dir, k) for k in (1, 2, 3)]
 
-    (near,) = call(
-        near_kernel,
-        [((32, 64, 128), F32)],
-        [near_list.T, near_count, before, flat, after, near_blocks],
-        [
-            pltpu.SMEM((6, 32), I32),
-            pltpu.SMEM((32,), I32),
-            pltpu.VMEM((97, 64, 256), BF16),
-            pltpu.VMEM((32, 6, 2, 64, 256), BF16),
-            pltpu.VMEM((32, 64, 128), F32),
-        ],
-        21,
-        SMALL,
-        "near",
-        limit=62,
-        landed=(2, 4),
-    )
     (fields,) = call(
         receive_kernel,
         [((32, 2, 32, 64), F32)],
-        [lowered] + shared + packed + [near],
+        [lowered] + shared + packed + near_parts,
         [
             pltpu.VMEM((4, 528, 128), I16),
             pltpu.VMEM((4, 1040, 128), I16),
@@ -663,7 +680,7 @@
             pltpu.VMEM((32, 64, 128), F32),
             pltpu.VMEM((32, 2, 32, 64), F32),
         ],
-        13,
+        14,
         LARGE,
         "receive",
         landed=(1, 2, 3, 5, 6, 7),

time: 86.6 us -> 87.1 us (level)
  waiting for transfers between devices: 10.2 us -> 4.6 us
  Pallas kernels: 32.2 us -> 35.6 us
  starting transfers between devices: 41.5 us -> 43.8 us
  local copies, waits for them, and re-layouts: 0.92 us -> 1.87 us
    all_to_all x1, starting transfers between devices: 4.99 us -> 8.77 us  [shards(): arrived = lax.all_to_all(moved.reshape(32, 16, 128), 'space', 0, 0)]
    pallas_call x8 -> x9, Pallas kernels: 32.2 us -> 35.6 us  [call(): pl.pallas_call(kernel, out_shape=shapes, in_specs=[ANYWHERE if n in lande...]
    all_to_all x1, waiting for transfers between devices: 3.26 us -> 0.92 us  [shards(): top = lax.all_to_all(message, 'space', 0, 0)]
    ppermute x9, starting transfers between devices: 15.9 us -> 13.8 us  [around(): return lax.ppermute(x, axis, [(i, (i + k) % peers) for i in range(peers)])]
    ppermute x1, waiting for transfers between devices: 2.01 us -> 0.01 us  [shards(): after = lax.ppermute(flat, 'space', down)]
    ppermute x1, starting transfers between devices: 4.73 us -> 3.2 us  [shards(): before = lax.ppermute(flat, 'space', up)]
    ppermute x1, starting transfers between devices: 1.92 us -> 3.45 us  [shards(): after = lax.ppermute(flat, 'space', down)]
    ppermute x1, waiting for transfers between devices: 3.6 us -> 2.48 us  [shards(): parents_after = lax.ppermute(halo, 'space', down)]
  transfers between devices with their start and end apart: 15 -> 15, of which waited for: 5 -> 3; matrix products, arithmetic and copies ran while one was open for 0% -> 0% of each run, Pallas kernels for 23% -> 27%
where the time goes in v1:
time: 87.1 us; the launch traced here: 86.3 us
  starting transfers between devices  43.8 us (50%)
  Pallas kernels  35.6 us (41%)
  waiting for transfers between devices  4.6 us (5%)
  local copies, waits for them, and re-layouts  1.87 us (2%)
    pallas_call x9, Pallas kernels, call(): pl.pallas_call(kernel, out_shape=shapes, in_specs=[ANYWHERE if n in lande...  35.6 us
    ppermute x9, starting transfers between devices, around(): return lax.ppermute(x, axis, [(i, (i + k) % peers) for i in range(peers)])  13.8 us
    all_to_all x1, starting transfers between devices, shards(): top = lax.all_to_all(message, 'space', 0, 0)  9.02 us
    all_to_all x1, starting transfers between devices, shards(): arrived = lax.all_to_all(moved.reshape(32, 16, 128), 'space', 0, 0)  8.77 us
    ppermute x1, starting transfers between devices, shards(): after = lax.ppermute(flat, 'space', down)  3.45 us
    ppermute x1, starting transfers between devices, shards(): parents_before = lax.ppermute(halo, 'space', up)  3.42 us
    ppermute x1, starting transfers between devices, shards(): before = lax.ppermute(flat, 'space', up)  3.2 us
    ppermute x1, waiting for transfers between devices, shards(): parents_after = lax.ppermute(halo, 'space', down)  2.48 us
  transfers between devices with their start and end apart: 15, of which 3 were waited for; matrix products, arithmetic and copies ran while one was open for 0% of the time, Pallas kernels for 27%

profile of v1, /device:TPU:1, one launch (start us, length us, event | category | flops | bytes accessed | tf_op | source)
XLA Modules:
  0.0 86.3 jit_solution(13881842519237053692)
XLA Ops:
  0.0 3.4 %collective-permute-start.4 = (bf16[32,64,256]{2,1,0:T(8,128)(2,1)}, bf16[32,64,256]{2,1,0:T(8,128)(2,1)S(1)}, u32[]{:S(2)}, u32[]{:S(2)}) collective-permute-start(bf16[32,64,256]{2,1,0:T(8,128)(2,1)} %bitcast.9), channel_id=1, source_target_pairs={{4,0},{8,4},{12,8},{16,12},{20,16},{24,20},{28,24},{32,28},{36,32}... | collective-permute-start | bytes 3145736 | tf_op jit(solution)/shard_map/ppermute | solution.py:539
  3.5 3.2 %collective-permute-start.3 = (bf16[32,64,256]{2,1,0:T(8,128)(2,1)}, bf16[32,64,256]{2,1,0:T(8,128)(2,1)}, u32[]{:S(2)}, u32[]{:S(2)}) collective-permute-start(bf16[32,64,256]{2,1,0:T(8,128)(2,1)} %bitcast.10), channel_id=1, source_target_pairs={{0,4},{4,8},{8,12},{12,16},{16,20},{20,24},{24,28},{28,32},{32,36}... | collective-permute-start | bytes 3145736 | tf_op jit(solution)/shard_map/ppermute | solution.py:538
  6.7 3.8 %leaf.1 = (s16[272,128]{1,0:T(8,128)(2,1)}, s16[272,128]{1,0:T(8,128)(2,1)}, s16[272,128]{1,0:T(8,128)(2,1)}, s16[272,128]{1,0:T(8,128)(2,1)}) custom-call(bf16[32,2,32,256]{3,2,1,0:T(8,128)(2,1)} %cur_from.1, bf16[32,2,32,256]{3,2,1,0:T(8,128)(2,1)} %rad_from.1, f32[40,2,128]{2,1,0:T(2,128)} %one_from.1, f32[40,2,512]{2,1,0:T(2,128)} %two_from.1), custom_call_target="tpu_custom_call" | custom-call | flops 68719476736 | bytes 68719476736 | tf_op jit(solution)/shard_map/leaf/pallas_call | solution.py:24
  10.5 1.7 %collective-permute-start = (s16[272,128]{1,0:T(8,128)(2,1)}, s16[272,128]{1,0:T(8,128)(2,1)S(1)}, u32[]{:S(2)}, u32[]{:S(2)}) collective-permute-start(s16[272,128]{1,0:T(8,128)(2,1)} %get-tuple-element.40), channel_id=1, source_target_pairs={{0,1},{1,2},{2,3},{3,0},{4,5},{5,6},{6,7},{7,4},{8,9},{9,10},{10,1... | collective-permute-start | bytes 208904 | tf_op jit(solution)/shard_map/ppermute | solution.py:507
  12.2 3.3 %collective-permute-start.1 = (s16[272,128]{1,0:T(8,128)(2,1)}, s16[272,128]{1,0:T(8,128)(2,1)S(1)}, u32[]{:S(2)}, u32[]{:S(2)}) collective-permute-start(s16[272,128]{1,0:T(8,128)(2,1)} %get-tuple-element.41), channel_id=1, source_target_pairs={{0,2},{1,3},{2,0},{3,1},{4,6},{5,7},{6,4},{7,5},{8,10},{9,11},{10,... | collective-permute-start | bytes 208904 | tf_op jit(solution)/shard_map/ppermute | solution.py:507
  16.2 3.1 %pack.1 = (s16[1040,128]{1,0:T(8,128)(2,1)S(1)}, s16[1040,128]{1,0:T(8,128)(2,1)S(1)}, s16[1040,128]{1,0:T(8,128)(2,1)S(1)}, s16[1040,128]{1,0:T(8,128)(2,1)S(1)...) custom-call(f32[32,2,32,256]{3,2,1,0:T(8,128)} %rec_from, ...), custom_call_target="tpu_custom_call" | custom-call | flops 4096 | bytes 4096 | tf_op jit(solution)/shard_map/pack/pallas_call | solution.py:24
  19.4 0.9 %copy-done.9 = bf16[32,64,256]{2,1,0:T(8,128)(2,1)} copy-done((bf16[32,64,256]{2,1,0:T(8,128)(2,1)}, bf16[32,64,256]{2,1,0:T(8,128)(2,1)S(1)}, u32[]{:S(2)}) %copy-start.9) | copy-done | bytes 1048600
  21.2 5.2 %lift.1 = (f32[8,2,8,512]{3,2,1,0:T(8,128)S(1)}, bf16[128,512]{1,0:T(8,128)(2,1)S(1)}, f32[32,16,128]{2,1,0:T(8,128)}) custom-call(s16[272,128]{1,0:T(8,128)(2,1)S(1)} %copy-done, s16[272,128]{1,0:T(8,128)(2,1)S(1)} %collective-permute-done.r1.m1, s16[272,128]{1,0:T(8,128)(2,1)S(1)} %collective-permute-done.1.r2.m2, ...), custom_call_target="tpu_custom_call" | custom-call | flops 68719476736 | bytes 68719476736 | tf_op jit(solution)/shard_map/lift/pallas_call | solution.py:24
  26.5 9.0 %all-to-all-start = ((f32[32,16,128]{2,1,0:T(8,128)}), f32[32,16,128]{2,1,0:T(8,128)S(1)}, u32[]{:S(2)}, u32[]{:S(2)}) async-start(f32[32,16,128]{2,1,0:T(8,128)} %get-tuple-element.58), calls=%async_computation | async-start | bytes 524288 | tf_op jit(solution)/shard_map/all_to_all | solution.py:602
  35.5 2.1 %collective-permute-start.6 = (bf16[128,512]{1,0:T(8,128)(2,1)S(1)}, bf16[128,512]{1,0:T(8,128)(2,1)S(1)}, u32[]{:S(2)}, u32[]{:S(2)}) collective-permute-start(bf16[128,512]{1,0:T(8,128)(2,1)S(1)} %get-tuple-element.59), channel_id=1, source_target_pairs={{4,0},{8,4},{12,8},{16,12},{20,16},{24,20},{28,24},{32,28},{36,32}... | collective-permute-start | bytes 393224 | tf_op jit(solution)/shard_map/ppermute | solution.py:604
  37.7 3.4 %collective-permute-start.5 = (bf16[128,512]{1,0:T(8,128)(2,1)S(1)}, bf16[128,512]{1,0:T(8,128)(2,1)S(1)}, u32[]{:S(2)}, u32[]{:S(2)}) collective-permute-start(bf16[128,512]{1,0:T(8,128)(2,1)S(1)} %get-tuple-element.59), channel_id=1, source_target_pairs={{0,4},{4,8},{8,12},{12,16},{16,20},{20,24},{24,28},{28,32},{32,36}... | collective-permute-start | bytes 393224 | tf_op jit(solution)/shard_map/ppermute | solution.py:603
  41.1 2.5 %collective-permute-done.6.after_from = bf16[128,512]{1,0:T(8,128)(2,1)S(1)} collective-permute-done((bf16[128,512]{1,0:T(8,128)(2,1)S(1)}, bf16[128,512]{1,0:T(8,128)(2,1)S(1)}, u32[]{:S(2)}, u32[]{:S(2)}) %collective-permute-start.6) | collective-permute-done | bytes 131104 | tf_op jit(solution)/shard_map/ppermute | solution.py:604
  43.6 0.9 %all-to-all-done = f32[32,16,128]{2,1,0:T(8,128)S(1)} async-done(((f32[32,16,128]{2,1,0:T(8,128)}), f32[32,16,128]{2,1,0:T(8,128)S(1)}, u32[]{:S(2)}, u32[]{:S(2)}) %all-to-all-start) | async-done | bytes 262176 | tf_op jit(solution)/shard_map/all_to_all | solution.py:602
  44.5 3.4 %translate_two.1 = f32[64,8,128]{2,1,0:T(8,128)} custom-call(s32[8,64]{1,0:T(8,128)S(1)} %bitcast.7, s32[8,64]{1,0:T(8,128)S(1)} %bitcast.8, f32[64,8,128]{2,1,0:T(8,128)S(1)} %bitcast.6, s16[272,128]{1,0:T(8,128)(2,1)S(1)} %copy-done.1, s16[272,128]{1,0:T(8,128)(2,1)S(1)} %collective-permute-done.r1.m1, s16[272,128]{1,0:T(8,128)(2,1)S(1)} %collective-permute-done.1.r2.m2, ...), custom_call_target="tpu_custom_call" | custom-call | flops 68719476736 | bytes 68719476736 | tf_op jit(solution)/shard_map/translate_two/pallas_call | solution.py:24
  47.9 8.8 %all-to-all-start.1 = ((f32[32,16,128]{2,1,0:T(8,128)}), f32[32,16,128]{2,1,0:T(8,128)S(1)}, u32[]{:S(2)}, u32[]{:S(2)}) async-start(f32[32,16,128]{2,1,0:T(8,128)} %bitcast.4), calls=%async_computation.1 | async-start | bytes 524288 | tf_op jit(solution)/shard_map/all_to_all | solution.py:625
  56.7 1.4 %collective-permute-start.10 = (s16[1040,128]{1,0:T(8,128)(2,1)S(1)}, s16[1040,128]{1,0:T(8,128)(2,1)S(1)}, u32[]{:S(2)}, u32[]{:S(2)}) collective-permute-start(s16[1040,128]{1,0:T(8,128)(2,1)S(1)} %get-tuple-element.69), channel_id=1, source_target_pairs={{0,1},{1,2},{2,3},{3,0},{4,5},{5,6},{6,7},{7,4},{8,9},{9,10},{10,1... | collective-permute-start | bytes 798728 | tf_op jit(solution)/shard_map/ppermute | solution.py:507
  58.1 3.3 %collective-permute-start.11 = (s16[1040,128]{1,0:T(8,128)(2,1)S(1)}, s16[1040,128]{1,0:T(8,128)(2,1)S(1)}, u32[]{:S(2)}, u32[]{:S(2)}) collective-permute-start(s16[1040,128]{1,0:T(8,128)(2,1)S(1)} %get-tuple-element.70), channel_id=1, source_target_pairs={{0,2},{1,3},{2,0},{3,1},{4,6},{5,7},{6,4},{7,5},{8,10},{9,11},{10,... | collective-permute-start | bytes 798728 | tf_op jit(solution)/shard_map/ppermute | solution.py:507
  62.1 5.6 %near.2.near_first = f32[16,64,128]{2,1,0:T(8,128)} custom-call(s32[6,32]{1,0:T(8,128)} %bitcast.13, s32[32]{0:T(128)} %counts_from.3, bf16[32,64,256]{2,1,0:T(8,128)(2,1)} %collective-permute-done.3.before, bf16[32,64,256]{2,1,0:T(8,128)(2,1)} %bitcast.11, bf16[32,64,256]{2,1,0:T(8,128)(2,1)} %copy-done.9, bf16[32,6,2,64,256]{4,3,2,1,0:T(8,128)(2,1)} %blocks_from.3), custom_call_target="tpu_custom_call" | custom-call | flops 4096 | bytes 4096 | tf_op jit(solution)/shard_map/near/pallas_call | solution.py:24
  67.7 1.2 %translate_one.1.near_one_from = f32[8,2,8,512]{3,2,1,0:T(8,128)S(1)} custom-call(s32[8,8]{1,0:T(8,128)S(1)} %copy-done.4, s32[8,8]{1,0:T(8,128)S(1)} %copy-done.5, bf16[128,512]{1,0:T(8,128)(2,1)S(1)} %collective-permute-done.5.before_from, f32[8,2,8,512]{3,2,1,0:T(8,128)S(1)} %get-tuple-element.62.parent_from, ...), custom_call_target="tpu_custom_call" | custom-call | flops 4096 | bytes 4096 | tf_op jit(solution)/shard_map/translate_one/pallas_call | solution.py:24
  68.9 3.8 %lower.1.l0 = s16[528,128]{1,0:T(8,128)(2,1)S(1)} custom-call(f32[32,16,128]{2,1,0:T(8,128)S(1)} %all-to-all-done.1.arrived_from, f32[8,2,8,512]{3,2,1,0:T(8,128)S(1)} %translate_one.1.near_one_from, f32[4,512]{1,0:T(4,128)S(1)} %get-tuple-element.54.refs_2_.refs_0_, f32[4,512]{1,0:T(4,128)S(1)} %get-tuple-element.55.refs_3_.refs_1_, ...), custom_call_target="tpu_custom_call" | custom-call | flops 68719476736 | bytes 68719476736 | tf_op jit(solution)/shard_map/lower/pallas_call | solution.py:24
  73.0 2.4 %collective-permute-start.8 = (s16[528,128]{1,0:T(8,128)(2,1)S(1)}, s16[528,128]{1,0:T(8,128)(2,1)S(1)}, u32[]{:S(2)}, u32[]{:S(2)}) collective-permute-start(s16[528,128]{1,0:T(8,128)(2,1)S(1)} %lower.1.l0), channel_id=1, source_target_pairs={{0,2},{1,3},{2,0},{3,1},{4,6},{5,7},{6,4},{7,5},{8,10},{9,11},{10,... | collective-permute-start | bytes 405512 | tf_op jit(solution)/shard_map/ppermute | solution.py:507
  75.4 5.6 %near.3.near_second = f32[16,64,128]{2,1,0:T(8,128)} custom-call(s32[6,32]{1,0:T(8,128)} %bitcast.14, s32[32]{0:T(128)} %counts_from.3, bf16[32,64,256]{2,1,0:T(8,128)(2,1)} %collective-permute-done.3.before, bf16[32,64,256]{2,1,0:T(8,128)(2,1)} %bitcast.12, bf16[32,64,256]{2,1,0:T(8,128)(2,1)} %copy-done.9, bf16[32,6,2,64,256]{4,3,2,1,0:T(8,128)(2,1)} %blocks_from.3), custom_call_target="tpu_custom_call" | custom-call | flops 4096 | bytes 4096 | tf_op jit(solution)/shard_map/near/pallas_call | solution.py:24
  81.0 1.2 %collective-permute-done.7.l1 = s16[528,128]{1,0:T(8,128)(2,1)S(1)} collective-permute-done((s16[528,128]{1,0:T(8,128)(2,1)S(1)}, s16[528,128]{1,0:T(8,128)(2,1)S(1)}, u32[]{:S(2)}, u32[]{:S(2)}) %collective-permute-start.7) | collective-permute-done | bytes 135200 | tf_op jit(solution)/shard_map/ppermute | solution.py:507
  82.1 4.0 %receive.1 = f32[32,2,32,64]{3,2,1,0:T(8,128)} custom-call(s16[528,128]{1,0:T(8,128)(2,1)S(1)} %lower.1.l0, s16[528,128]{1,0:T(8,128)(2,1)S(1)} %collective-permute-done.7.l1, s16[528,128]{1,0:T(8,128)(2,1)S(1)} %collective-permute-done.8.l2, s16[528,128]{1,0:T(8,128)(2,1)S(1)} %collective-permute-done.9.l3, s16[1040,128]{1,0:T(8,128)(2,1)S(1)} %get-tuple-element.68.x0, ...), custom_call_target="tpu_custom_call" | custom-call | flops 68719476736 | bytes 68719476736 | tf_op jit(solution)/shard_map/receive/pallas_call | solution.py:24
  (35 shorter events, 2.7 us)
Async XLA Ops:
  0.0 16.2 %copy-start.2 = (f32[4,2048]{1,0:T(4,128)S(1)}, f32[4,2048]{1,0:T(4,128)}, u32[]{:S(2)}) copy-start(f32[4,2048]{1,0:T(4,128)} %two_from.2) | copy-start | bytes 98308
  0.0 16.2 %copy-start.3 = (f32[4,512]{1,0:T(4,128)S(1)}, f32[4,512]{1,0:T(4,128)}, u32[]{:S(2)}) copy-start(f32[4,512]{1,0:T(4,128)} %one_from.2) | copy-start | bytes 24580
  0.0 20.3 %copy-start.6 = (f32[512,128]{1,0:T(8,128)S(1)}, f32[512,128]{1,0:T(8,128)}, u32[]{:S(2)}) copy-start(f32[512,128]{1,0:T(8,128)} %refs_4_.1) | copy-start | bytes 786436
  0.0 19.4 %collective-permute-start.4 = (bf16[32,64,256]{2,1,0:T(8,128)(2,1)}, bf16[32,64,256]{2,1,0:T(8,128)(2,1)S(1)}, u32[]{:S(2)}, u32[]{:S(2)}) collective-permute-start(bf16[32,64,256]{2,1,0:T(8,128)(2,1)} %bitcast.9), channel_id=1, source_target_pairs={{4,0},{8,4},{12,8},{16,12},{20,16},{24,20},{28,24},{32,28},{36,32}... | collective-permute-start | bytes 3145736 | tf_op jit(solution)/shard_map/ppermute | solution.py:539
  3.5 15.9 %collective-permute-start.3 = (bf16[32,64,256]{2,1,0:T(8,128)(2,1)}, bf16[32,64,256]{2,1,0:T(8,128)(2,1)}, u32[]{:S(2)}, u32[]{:S(2)}) collective-permute-start(bf16[32,64,256]{2,1,0:T(8,128)(2,1)} %bitcast.10), channel_id=1, source_target_pairs={{0,4},{4,8},{8,12},{12,16},{16,20},{20,24},{24,28},{28,32},{32,36}... | collective-permute-start | bytes 3145736 | tf_op jit(solution)/shard_map/ppermute | solution.py:538
  10.5 8.8 %collective-permute-start = (s16[272,128]{1,0:T(8,128)(2,1)}, s16[272,128]{1,0:T(8,128)(2,1)S(1)}, u32[]{:S(2)}, u32[]{:S(2)}) collective-permute-start(s16[272,128]{1,0:T(8,128)(2,1)} %get-tuple-element.40), channel_id=1, source_target_pairs={{0,1},{1,2},{2,3},{3,0},{4,5},{5,6},{6,7},{7,4},{8,9},{9,10},{10,1... | collective-permute-start | bytes 208904 | tf_op jit(solution)/shard_map/ppermute | solution.py:507
  12.2 7.1 %collective-permute-start.1 = (s16[272,128]{1,0:T(8,128)(2,1)}, s16[272,128]{1,0:T(8,128)(2,1)S(1)}, u32[]{:S(2)}, u32[]{:S(2)}) collective-permute-start(s16[272,128]{1,0:T(8,128)(2,1)} %get-tuple-element.41), channel_id=1, source_target_pairs={{0,2},{1,3},{2,0},{3,1},{4,6},{5,7},{6,4},{7,5},{8,10},{9,11},{10,... | collective-permute-start | bytes 208904 | tf_op jit(solution)/shard_map/ppermute | solution.py:507
  15.5 3.9 %collective-permute-start.2 = (s16[272,128]{1,0:T(8,128)(2,1)}, s16[272,128]{1,0:T(8,128)(2,1)S(1)}, u32[]{:S(2)}, u32[]{:S(2)}) collective-permute-start(s16[272,128]{1,0:T(8,128)(2,1)} %get-tuple-element.42), channel_id=1, source_target_pairs={{0,3},{1,0},{2,1},{3,2},{4,7},{5,4},{6,5},{7,6},{8,11},{9,8},{10,9... | collective-permute-start | bytes 208904 | tf_op jit(solution)/shard_map/ppermute | solution.py:507
  19.4 1.0 %copy-start.9 = (bf16[32,64,256]{2,1,0:T(8,128)(2,1)}, bf16[32,64,256]{2,1,0:T(8,128)(2,1)S(1)}, u32[]{:S(2)}) copy-start(bf16[32,64,256]{2,1,0:T(8,128)(2,1)S(1)} %collective-permute-done.4.after) | copy-start | bytes 3145732
  21.2 23.3 %copy-start.1 = (s16[272,128]{1,0:T(8,128)(2,1)S(1)}, s16[272,128]{1,0:T(8,128)(2,1)}, u32[]{:S(2)}) copy-start(s16[272,128]{1,0:T(8,128)(2,1)} %get-tuple-element.50.r0.m0) | copy-start | bytes 208900
  21.2 23.3 %copy-start.7 = (s32[64,8]{0,1:T(8,128)S(1)}, s32[64,8]{0,1:T(8,128)}, u32[]{:S(2)}) copy-start(s32[64,8]{0,1:T(8,128)} %param.30) | copy-start | bytes 6148
  21.2 23.3 %copy-start.8 = (s32[64,8]{0,1:T(8,128)S(1)}, s32[64,8]{0,1:T(8,128)}, u32[]{:S(2)}) copy-start(s32[64,8]{0,1:T(8,128)} %param.31) | copy-start | bytes 6148
  26.5 18.0 %all-to-all-start = ((f32[32,16,128]{2,1,0:T(8,128)}), f32[32,16,128]{2,1,0:T(8,128)S(1)}, u32[]{:S(2)}, u32[]{:S(2)}) async-start(f32[32,16,128]{2,1,0:T(8,128)} %get-tuple-element.58), calls=%async_computation | async-start | bytes 524288 | tf_op jit(solution)/shard_map/all_to_all | solution.py:602
  35.5 8.1 %collective-permute-start.6 = (bf16[128,512]{1,0:T(8,128)(2,1)S(1)}, bf16[128,512]{1,0:T(8,128)(2,1)S(1)}, u32[]{:S(2)}, u32[]{:S(2)}) collective-permute-start(bf16[128,512]{1,0:T(8,128)(2,1)S(1)} %get-tuple-element.59), channel_id=1, source_target_pairs={{4,0},{8,4},{12,8},{16,12},{20,16},{24,20},{28,24},{32,28},{36,32}... | collective-permute-start | bytes 393224 | tf_op jit(solution)/shard_map/ppermute | solution.py:604
  37.7 5.9 %collective-permute-start.5 = (bf16[128,512]{1,0:T(8,128)(2,1)S(1)}, bf16[128,512]{1,0:T(8,128)(2,1)S(1)}, u32[]{:S(2)}, u32[]{:S(2)}) collective-permute-start(bf16[128,512]{1,0:T(8,128)(2,1)S(1)} %get-tuple-element.59), channel_id=1, source_target_pairs={{0,4},{4,8},{8,12},{12,16},{16,20},{20,24},{24,28},{28,32},{32,36}... | collective-permute-start | bytes 393224 | tf_op jit(solution)/shard_map/ppermute | solution.py:603
  47.9 21.0 %all-to-all-start.1 = ((f32[32,16,128]{2,1,0:T(8,128)}), f32[32,16,128]{2,1,0:T(8,128)S(1)}, u32[]{:S(2)}, u32[]{:S(2)}) async-start(f32[32,16,128]{2,1,0:T(8,128)} %bitcast.4), calls=%async_computation.1 | async-start | bytes 524288 | tf_op jit(solution)/shard_map/all_to_all | solution.py:625
  56.7 18.7 %collective-permute-start.10 = (s16[1040,128]{1,0:T(8,128)(2,1)S(1)}, s16[1040,128]{1,0:T(8,128)(2,1)S(1)}, u32[]{:S(2)}, u32[]{:S(2)}) collective-permute-start(s16[1040,128]{1,0:T(8,128)(2,1)S(1)} %get-tuple-element.69), channel_id=1, source_target_pairs={{0,1},{1,2},{2,3},{3,0},{4,5},{5,6},{6,7},{7,4},{8,9},{9,10},{10,1... | collective-permute-start | bytes 798728 | tf_op jit(solution)/shard_map/ppermute | solution.py:507
  58.1 22.9 %collective-permute-start.11 = (s16[1040,128]{1,0:T(8,128)(2,1)S(1)}, s16[1040,128]{1,0:T(8,128)(2,1)S(1)}, u32[]{:S(2)}, u32[]{:S(2)}) collective-permute-start(s16[1040,128]{1,0:T(8,128)(2,1)S(1)} %get-tuple-element.70), channel_id=1, source_target_pairs={{0,2},{1,3},{2,0},{3,1},{4,6},{5,7},{6,4},{7,5},{8,10},{9,11},{10,... | collective-permute-start | bytes 798728 | tf_op jit(solution)/shard_map/ppermute | solution.py:507
  61.4 19.6 %collective-permute-start.12 = (s16[1040,128]{1,0:T(8,128)(2,1)S(1)}, s16[1040,128]{1,0:T(8,128)(2,1)S(1)}, u32[]{:S(2)}, u32[]{:S(2)}) collective-permute-start(s16[1040,128]{1,0:T(8,128)(2,1)S(1)} %get-tuple-element.71), channel_id=1, source_target_pairs={{0,3},{1,0},{2,1},{3,2},{4,7},{5,4},{6,5},{7,6},{8,11},{9,8},{10,9... | collective-permute-start | bytes 798728 | tf_op jit(solution)/shard_map/ppermute | solution.py:507
  62.1 5.6 %copy-start.4 = (s32[8,8]{1,0:T(8,128)S(1)}, s32[8,8]{1,0:T(8,128)}, u32[]{:S(2)}) copy-start(s32[8,8]{1,0:T(8,128)} %kinds_from.1) | copy-start | bytes 772
  62.1 5.6 %copy-start.5 = (s32[8,8]{1,0:T(8,128)S(1)}, s32[8,8]{1,0:T(8,128)}, u32[]{:S(2)}) copy-start(s32[8,8]{1,0:T(8,128)} %lists_from.1) | copy-start | bytes 772
  72.7 8.2 %collective-permute-start.9 = (s16[528,128]{1,0:T(8,128)(2,1)S(1)}, s16[528,128]{1,0:T(8,128)(2,1)S(1)}, u32[]{:S(2)}, u32[]{:S(2)}) collective-permute-start(s16[528,128]{1,0:T(8,128)(2,1)S(1)} %lower.1.l0), channel_id=1, source_target_pairs={{0,3},{1,0},{2,1},{3,2},{4,7},{5,4},{6,5},{7,6},{8,11},{9,8},{10,9... | collective-permute-start | bytes 405512 | tf_op jit(solution)/shard_map/ppermute | solution.py:507
  73.0 8.0 %collective-permute-start.8 = (s16[528,128]{1,0:T(8,128)(2,1)S(1)}, s16[528,128]{1,0:T(8,128)(2,1)S(1)}, u32[]{:S(2)}, u32[]{:S(2)}) collective-permute-start(s16[528,128]{1,0:T(8,128)(2,1)S(1)} %lower.1.l0), channel_id=1, source_target_pairs={{0,2},{1,3},{2,0},{3,1},{4,6},{5,7},{6,4},{7,5},{8,10},{9,11},{10,... | collective-permute-start | bytes 405512 | tf_op jit(solution)/shard_map/ppermute | solution.py:507
  75.4 6.8 %collective-permute-start.7 = (s16[528,128]{1,0:T(8,128)(2,1)S(1)}, s16[528,128]{1,0:T(8,128)(2,1)S(1)}, u32[]{:S(2)}, u32[]{:S(2)}) collective-permute-start(s16[528,128]{1,0:T(8,128)(2,1)S(1)} %lower.1.l0), channel_id=1, source_target_pairs={{0,1},{1,2},{2,3},{3,0},{4,5},{5,6},{6,7},{7,4},{8,9},{9,10},{10,1... | collective-permute-start | bytes 405512 | tf_op jit(solution)/shard_map/ppermute | solution.py:507
  (1 other events, 0.9 us)

commit v2 on v0

--- a/solution.py
+++ b/solution.py
@@ -302,26 +302,27 @@
 
 
 def parent_kernel(
-    kinds_from, lists_from, before_from, parent_from, after_from, m0, m1, m2, m3,
+    kinds_from, lists_from, inner_from, parent_from, outer_from, m0, m1, m2, m3,
     out_to,
-    kinds, lists, before, after, held, codes, table, out, sems,
+    kinds, lists, inner, outer, held, codes, table, out, sems,
 ):
     finish(
         *begin(
             sems,
             (kinds_from, kinds),
             (lists_from, lists),
-            (before_from, before),
+            (inner_from, inner),
             (parent_from, held.at[8:16]),
-            (after_from, after),
+            (outer_from, outer),
             *[(m.at[176:272], codes.at[sender(k)]) for k, m in enumerate((m0, m1, m2, m3))],
         )
     )
     base = lax.axis_index("space") * 8 - 8
     for e in range(4):
         table[e] = value_of(codes[e, 0:80]) * unit_from(value_of(codes[e, 80:96])[2:3])
-    held[0:8] = before[...].astype(F32).reshape(8, 2, 8, 512)
-    held[16:24] = after[...].astype(F32).reshape(8, 2, 8, 512)
+    odd = lax.rem(lax.axis_index("space"), 2)
+    held[pl.ds(16 - 16 * odd, 8)] = inner[...].astype(F32).reshape(8, 2, 8, 512)
+    held[pl.ds(16 * odd, 8)] = outer[...].astype(F32).reshape(8, 2, 8, 512)
 
     def body(p, carry):
         re = [jnp.zeros((8, 128), F32) for _ in range(4)]
@@ -401,14 +402,15 @@
     finish(*begin(sems, (out, out_to)))
 
 
-def near_kernel(lists_from, counts_from, before, current, after, blocks_from, out_to, lists, counts, held, blocks, out, sems):
+def near_kernel(lists_from, counts_from, inner, current, outer, blocks_from, out_to, lists, counts, held, blocks, out, sems):
+    odd = lax.rem(lax.axis_index("space"), 2)
     copies = begin(
         sems,
         (lists_from, lists),
         (counts_from, counts),
-        (before, held.at[0:32]),
+        (inner, held.at[pl.ds(64 - 64 * odd, 32)]),
         (current, held.at[32:64]),
-        (after, held.at[64:96]),
+        (outer, held.at[pl.ds(64 * odd, 32)]),
         *[(blocks_from.at[4 * t : 4 * t + 4], blocks.at[4 * t : 4 * t + 4]) for t in range(8)],
     )
     held[96] = jnp.zeros((64, 256), BF16)
@@ -500,12 +502,12 @@
 ):
     n_space = lax.axis_size("space")
     n_dir = lax.axis_size("dir")
-    up = [(i, i + 1) for i in range(n_space - 1)]
-    down = [(i + 1, i) for i in range(n_space - 1)]
+    first_swap = [(i ^ 1, i) for i in range(n_space)]
+    second_swap = [(i, j) for k in range(1, n_space - 1, 2) for i, j in ((k, k + 1), (k + 1, k))]
 
     flat = currents.reshape(32, 64, 256)
-    before = lax.ppermute(flat, "space", up)
-    after = lax.ppermute(flat, "space", down)
+    inner = lax.ppermute(flat, "space", first_swap)
+    outer = lax.ppermute(flat, "space", second_swap)
 
     leaf = call(
         leaf_kernel,
@@ -543,7 +545,7 @@
         "pack",
     )
     packed, angles = packed[:4], packed[4:]
-    leaf, packed, before, after = lax.optimization_barrier((leaf, packed, before, after))
+    leaf, packed = lax.optimization_barrier((leaf, packed))
     packed = [packed[0]] + [around(packed[k], "dir", n_dir, k) for k in (1, 2, 3)]
 
 
@@ -568,9 +570,10 @@
         landed=(1, 2, 3),
     )
     top = lax.all_to_all(message, "space", 0, 0)
-    parents_before = lax.ppermute(halo, "space", up)
-    parents_after = lax.ppermute(halo, "space", down)
-
+    parents_inner = lax.ppermute(halo, "space", first_swap)
+    parents_outer = lax.ppermute(halo, "space", second_swap)
+
+    top, inner, outer = lax.optimization_barrier((top, inner, outer))
     (moved,) = call(
         top_kernel,
         [((64, 8, 128), F32)],
@@ -591,11 +594,11 @@
     )
     arrived = lax.all_to_all(moved.reshape(32, 16, 128), "space", 0, 0)
 
-    packed, parents_before, parents_after = lax.optimization_barrier((packed, parents_before, parents_after))
+    packed, parents_inner, parents_outer = lax.optimization_barrier((packed, parents_inner, parents_outer))
     (near_one,) = call(
         parent_kernel,
         [((8, 2, 8, 512), F32)],
-        [kind_one, list_one, parents_before, parent, parents_after] + leaf,
+        [kind_one, list_one, parents_inner, parent, parents_outer] + leaf,
         [
             pltpu.SMEM((8, 8), I32),
             pltpu.SMEM((8, 8), I32),
@@ -637,7 +640,7 @@
     (near,) = call(
         near_kernel,
         [((32, 64, 128), F32)],
-        [near_list.T, near_count, before, flat, after, near_blocks],
+        [near_list.T, near_count, inner, flat, outer, near_blocks],
         [
             pltpu.SMEM((6, 32), I32),
             pltpu.SMEM((32,), I32),

time: 86.6 us -> 76.3 us (0.88)
  starting transfers between devices: 41.5 us -> 31.8 us
    ppermute x4, starting transfers between devices: 12.1 us -> 8.32 us  [the longest x1 4.6 us: shards(): outer = lax.ppermute(flat, 'space', second_swap)]
    ppermute x9, starting transfers between devices: 15.9 us -> 12.5 us  [around(): return lax.ppermute(x, axis, [(i, (i + k) % peers) for i in range(peers)])]
    all_to_all x1, waiting for transfers between devices: 3.26 us -> 5.69 us  [shards(): top = lax.all_to_all(message, 'space', 0, 0)]
    ppermute x4, waiting for transfers between devices: 6.37 us -> 4.52 us  [the longest x1 4.52 us: shards(): parents_outer = lax.ppermute(halo, 'space', second_swap)]
    all_to_all x1, starting transfers between devices: 4.99 us -> 3.72 us  [shards(): arrived = lax.all_to_all(moved.reshape(32, 16, 128), 'space', 0, 0)]
    all_to_all x1, starting transfers between devices: 8.43 us -> 7.26 us  [shards(): top = lax.all_to_all(message, 'space', 0, 0)]
  transfers between devices with their start and end apart: 15 -> 15, of which waited for: 5 -> 2; matrix products, arithmetic and copies ran while one was open for 0% -> 0% of each run, Pallas kernels for 23% -> 28%
where the time goes in v2:
time: 76.3 us; the launch traced here: 75.6 us
  Pallas kernels  32.3 us (42%)
  starting transfers between devices  31.8 us (42%)
  waiting for transfers between devices  10.2 us (13%)
  local copies, waits for them, and re-layouts  0.91 us (1%)
    pallas_call x8, Pallas kernels, call(): pl.pallas_call(kernel, out_shape=shapes, in_specs=[ANYWHERE if n in lande...  32.3 us
    ppermute x9, starting transfers between devices, around(): return lax.ppermute(x, axis, [(i, (i + k) % peers) for i in range(peers)])  12.5 us
    all_to_all x1, starting transfers between devices, shards(): top = lax.all_to_all(message, 'space', 0, 0)  7.26 us
    all_to_all x1, waiting for transfers between devices, shards(): top = lax.all_to_all(message, 'space', 0, 0)  5.69 us
    ppermute x1, starting transfers between devices, shards(): outer = lax.ppermute(flat, 'space', second_swap)  4.6 us
    ppermute x1, waiting for transfers between devices, shards(): parents_outer = lax.ppermute(halo, 'space', second_swap)  4.52 us
    all_to_all x1, starting transfers between devices, shards(): arrived = lax.all_to_all(moved.reshape(32, 16, 128), 'space', 0, 0)  3.72 us
    ppermute x1, starting transfers between devices, shards(): parents_outer = lax.ppermute(halo, 'space', second_swap)  3.55 us
  transfers between devices with their start and end apart: 15, of which 2 were waited for; matrix products, arithmetic and copies ran while one was open for 0% of the time, Pallas kernels for 28%

profile of v2, /device:TPU:1, one launch (start us, length us, event | category | flops | bytes accessed | tf_op | source)
XLA Modules:
  0.0 75.6 jit_solution(17599423305481224367)
XLA Ops:
  0.0 3.2 %leaf.1 = (s16[272,128]{1,0:T(8,128)(2,1)}, s16[272,128]{1,0:T(8,128)(2,1)}, s16[272,128]{1,0:T(8,128)(2,1)}, s16[272,128]{1,0:T(8,128)(2,1)}) custom-call(bf16[32,2,32,256]{3,2,1,0:T(8,128)(2,1)} %cur_from.1, bf16[32,2,32,256]{3,2,1,0:T(8,128)(2,1)} %rad_from.1, f32[40,2,128]{2,1,0:T(2,128)} %one_from.1, f32[40,2,512]{2,1,0:T(2,128)} %two_from.1), custom_call_target="tpu_custom_call" | custom-call | flops 68719476736 | bytes 68719476736 | tf_op jit(solution)/shard_map/leaf/pallas_call | solution.py:21
  3.2 2.5 %collective-permute-start = (s16[272,128]{1,0:T(8,128)(2,1)}, s16[272,128]{1,0:T(8,128)(2,1)S(1)}, u32[]{:S(2)}, u32[]{:S(2)}) collective-permute-start(s16[272,128]{1,0:T(8,128)(2,1)} %get-tuple-element.41), channel_id=1, source_target_pairs={{0,1},{1,2},{2,3},{3,0},{4,5},{5,6},{6,7},{7,4},{8,9},{9,10},{10,1... | collective-permute-start | bytes 208904 | tf_op jit(solution)/shard_map/ppermute | solution.py:478
  5.7 3.3 %collective-permute-start.1 = (s16[272,128]{1,0:T(8,128)(2,1)}, s16[272,128]{1,0:T(8,128)(2,1)S(1)}, u32[]{:S(2)}, u32[]{:S(2)}) collective-permute-start(s16[272,128]{1,0:T(8,128)(2,1)} %get-tuple-element.42), channel_id=1, source_target_pairs={{0,2},{1,3},{2,0},{3,1},{4,6},{5,7},{6,4},{7,5},{8,10},{9,11},{10,... | collective-permute-start | bytes 208904 | tf_op jit(solution)/shard_map/ppermute | solution.py:478
  9.0 0.7 collective-permute-start.2
  9.7 4.6 %collective-permute-start.4 = (bf16[32,64,256]{2,1,0:T(8,128)(2,1)}, bf16[32,64,256]{2,1,0:T(8,128)(2,1)}, u32[]{:S(2)}, u32[]{:S(2)}) collective-permute-start(bf16[32,64,256]{2,1,0:T(8,128)(2,1)} %bitcast.2.current), channel_id=1, source_target_pairs={{4,8},{8,4},{12,16},{16,12},{20,24},{24,20},{28,32},{32,28},{36,40... | collective-permute-start | bytes 3145736 | tf_op jit(solution)/shard_map/ppermute | solution.py:510
  14.3 0.1 collective-permute-start.3
  14.5 3.1 %pack.1 = (s16[1040,128]{1,0:T(8,128)(2,1)S(1)}, s16[1040,128]{1,0:T(8,128)(2,1)S(1)}, s16[1040,128]{1,0:T(8,128)(2,1)S(1)}, s16[1040,128]{1,0:T(8,128)(2,1)S(1)...) custom-call(f32[32,2,32,256]{3,2,1,0:T(8,128)} %rec_from, ...), custom_call_target="tpu_custom_call" | custom-call | flops 4096 | bytes 4096 | tf_op jit(solution)/shard_map/pack/pallas_call | solution.py:21
  17.6 0.9 %copy-done = s16[272,128]{1,0:T(8,128)(2,1)S(1)} copy-done((s16[272,128]{1,0:T(8,128)(2,1)S(1)}, s16[272,128]{1,0:T(8,128)(2,1)}, u32[]{:S(2)}) %copy-start) | copy-done | bytes 69656
  18.5 5.3 %lift.1 = (f32[8,2,8,512]{3,2,1,0:T(8,128)S(1)}, bf16[128,512]{1,0:T(8,128)(2,1)S(1)}, f32[32,16,128]{2,1,0:T(8,128)}) custom-call(s16[272,128]{1,0:T(8,128)(2,1)S(1)} %copy-done, s16[272,128]{1,0:T(8,128)(2,1)S(1)} %collective-permute-done.r1.m1, s16[272,128]{1,0:T(8,128)(2,1)S(1)} %collective-permute-done.1.r2.m2, ...), custom_call_target="tpu_custom_call" | custom-call | flops 68719476736 | bytes 68719476736 | tf_op jit(solution)/shard_map/lift/pallas_call | solution.py:21
  23.8 7.3 %all-to-all-start = ((f32[32,16,128]{2,1,0:T(8,128)}), f32[32,16,128]{2,1,0:T(8,128)S(1)}, u32[]{:S(2)}, u32[]{:S(2)}) async-start(f32[32,16,128]{2,1,0:T(8,128)} %get-tuple-element.59), calls=%async_computation | async-start | bytes 524288 | tf_op jit(solution)/shard_map/all_to_all | solution.py:572
  31.0 0.8 %collective-permute-start.5 = (s16[1040,128]{1,0:T(8,128)(2,1)S(1)}, s16[1040,128]{1,0:T(8,128)(2,1)S(1)}, u32[]{:S(2)}, u32[]{:S(2)}) collective-permute-start(s16[1040,128]{1,0:T(8,128)(2,1)S(1)} %get-tuple-element.62), channel_id=1, source_target_pairs={{0,1},{1,2},{2,3},{3,0},{4,5},{5,6},{6,7},{7,4},{8,9},{9,10},{10,1... | collective-permute-start | bytes 798728 | tf_op jit(solution)/shard_map/ppermute | solution.py:478
  31.8 0.2 collective-permute-start.6
  32.0 2.3 %collective-permute-start.7 = (s16[1040,128]{1,0:T(8,128)(2,1)S(1)}, s16[1040,128]{1,0:T(8,128)(2,1)S(1)}, u32[]{:S(2)}, u32[]{:S(2)}) collective-permute-start(s16[1040,128]{1,0:T(8,128)(2,1)S(1)} %get-tuple-element.64), channel_id=1, source_target_pairs={{0,3},{1,0},{2,1},{3,2},{4,7},{5,4},{6,5},{7,6},{8,11},{9,8},{10,9... | collective-permute-start | bytes 798728 | tf_op jit(solution)/shard_map/ppermute | solution.py:478
  34.3 5.7 %all-to-all-done = f32[32,16,128]{2,1,0:T(8,128)S(1)} async-done(((f32[32,16,128]{2,1,0:T(8,128)}), f32[32,16,128]{2,1,0:T(8,128)S(1)}, u32[]{:S(2)}, u32[]{:S(2)}) %all-to-all-start) | async-done | bytes 262176 | tf_op jit(solution)/shard_map/all_to_all | solution.py:572
  40.1 3.4 %translate_two.1 = f32[64,8,128]{2,1,0:T(8,128)} custom-call(s32[8,64]{1,0:T(8,128)S(1)} %bitcast.7, s32[8,64]{1,0:T(8,128)S(1)} %bitcast.8, f32[64,8,128]{2,1,0:T(8,128)S(1)} %bitcast.6, s16[272,128]{1,0:T(8,128)(2,1)S(1)} %copy-done.1, s16[272,128]{1,0:T(8,128)(2,1)S(1)} %collective-permute-done.r1.m1, s16[272,128]{1,0:T(8,128)(2,1)S(1)} %collective-permute-done.1.r2.m2, ...), custom_call_target="tpu_custom_call" | custom-call | flops 68719476736 | bytes 68719476736 | tf_op jit(solution)/shard_map/translate_two/pallas_call | solution.py:21
  43.5 3.7 %all-to-all-start.1 = ((f32[32,16,128]{2,1,0:T(8,128)}), f32[32,16,128]{2,1,0:T(8,128)S(1)}, u32[]{:S(2)}, u32[]{:S(2)}) async-start(f32[32,16,128]{2,1,0:T(8,128)} %bitcast.4), calls=%async_computation.1 | async-start | bytes 524288 | tf_op jit(solution)/shard_map/all_to_all | solution.py:595
  47.2 3.5 %collective-permute-start.9 = (bf16[128,512]{1,0:T(8,128)(2,1)S(1)}, bf16[128,512]{1,0:T(8,128)(2,1)S(1)}, u32[]{:S(2)}, u32[]{:S(2)}) collective-permute-start(bf16[128,512]{1,0:T(8,128)(2,1)S(1)} %get-tuple-element.65), channel_id=1, source_target_pairs={{4,8},{8,4},{12,16},{16,12},{20,24},{24,20},{28,32},{32,28},{36,40... | collective-permute-start | bytes 393224 | tf_op jit(solution)/shard_map/ppermute | solution.py:574
  50.7 0.1 collective-permute-start.8
  50.8 4.5 %collective-permute-done.9.outer_from = bf16[128,512]{1,0:T(8,128)(2,1)S(1)} collective-permute-done((bf16[128,512]{1,0:T(8,128)(2,1)S(1)}, bf16[128,512]{1,0:T(8,128)(2,1)S(1)}, u32[]{:S(2)}, u32[]{:S(2)}) %collective-permute-start.9) | collective-permute-done | bytes 131104 | tf_op jit(solution)/shard_map/ppermute | solution.py:574
  55.4 1.2 %translate_one.1.near_one_from = f32[8,2,8,512]{3,2,1,0:T(8,128)S(1)} custom-call(s32[8,8]{1,0:T(8,128)S(1)} %copy-done.4, s32[8,8]{1,0:T(8,128)S(1)} %copy-done.5, bf16[128,512]{1,0:T(8,128)(2,1)S(1)} %collective-permute-done.8.inner_from, f32[8,2,8,512]{3,2,1,0:T(8,128)S(1)} %get-tuple-element.67.parent_from, ...), custom_call_target="tpu_custom_call" | custom-call | flops 4096 | bytes 4096 | tf_op jit(solution)/shard_map/translate_one/pallas_call | solution.py:21
  56.6 3.8 %lower.1.l0 = s16[528,128]{1,0:T(8,128)(2,1)S(1)} custom-call(f32[32,16,128]{2,1,0:T(8,128)S(1)} %all-to-all-done.1.arrived_from, f32[8,2,8,512]{3,2,1,0:T(8,128)S(1)} %translate_one.1.near_one_from, f32[4,512]{1,0:T(4,128)S(1)} %get-tuple-element.55.refs_2_.refs_0_, f32[4,512]{1,0:T(4,128)S(1)} %get-tuple-element.56.refs_3_.refs_1_, ...), custom_call_target="tpu_custom_call" | custom-call | flops 68719476736 | bytes 68719476736 | tf_op jit(solution)/shard_map/lower/pallas_call | solution.py:21
  60.5 2.5 %collective-permute-start.11 = (s16[528,128]{1,0:T(8,128)(2,1)S(1)}, s16[528,128]{1,0:T(8,128)(2,1)S(1)}, u32[]{:S(2)}, u32[]{:S(2)}) collective-permute-start(s16[528,128]{1,0:T(8,128)(2,1)S(1)} %lower.1.l0), channel_id=1, source_target_pairs={{0,2},{1,3},{2,0},{3,1},{4,6},{5,7},{6,4},{7,5},{8,10},{9,11},{10,... | collective-permute-start | bytes 405512 | tf_op jit(solution)/shard_map/ppermute | solution.py:478
  63.0 8.4 %near.1.near_from = f32[32,64,128]{2,1,0:T(8,128)} custom-call(s32[6,32]{1,0:T(8,128)} %bitcast.9, s32[32]{0:T(128)} %counts_from.1, bf16[32,64,256]{2,1,0:T(8,128)(2,1)} %collective-permute-done.3.inner, bf16[32,64,256]{2,1,0:T(8,128)(2,1)} %bitcast.2.current, bf16[32,64,256]{2,1,0:T(8,128)(2,1)} %collective-permute-done.4.outer, ...), custom_call_target="tpu_custom_call" | custom-call | flops 4096 | bytes 4096 | tf_op jit(solution)/shard_map/near/pallas_call | solution.py:21
  71.5 4.0 %receive.1 = f32[32,2,32,64]{3,2,1,0:T(8,128)} custom-call(s16[528,128]{1,0:T(8,128)(2,1)S(1)} %lower.1.l0, s16[528,128]{1,0:T(8,128)(2,1)S(1)} %collective-permute-done.10.l1, s16[528,128]{1,0:T(8,128)(2,1)S(1)} %collective-permute-done.11.l2, s16[528,128]{1,0:T(8,128)(2,1)S(1)} %collective-permute-done.12.l3, s16[1040,128]{1,0:T(8,128)(2,1)S(1)} %get-tuple-element.69.x0, ...), custom_call_target="tpu_custom_call" | custom-call | flops 68719476736 | bytes 68719476736 | tf_op jit(solution)/shard_map/receive/pallas_call | solution.py:21
  (32 shorter events, 0.1 us)
Async XLA Ops:
  0.0 14.4 %copy-start.2 = (f32[4,2048]{1,0:T(4,128)S(1)}, f32[4,2048]{1,0:T(4,128)}, u32[]{:S(2)}) copy-start(f32[4,2048]{1,0:T(4,128)} %two_from.2) | copy-start | bytes 98308
  0.0 14.4 %copy-start.3 = (f32[4,512]{1,0:T(4,128)S(1)}, f32[4,512]{1,0:T(4,128)}, u32[]{:S(2)}) copy-start(f32[4,512]{1,0:T(4,128)} %one_from.2) | copy-start | bytes 24580
  0.0 17.6 %copy-start.6 = (f32[512,128]{1,0:T(8,128)S(1)}, f32[512,128]{1,0:T(8,128)}, u32[]{:S(2)}) copy-start(f32[512,128]{1,0:T(8,128)} %refs_4_.1) | copy-start | bytes 786436
  3.2 14.4 %collective-permute-start = (s16[272,128]{1,0:T(8,128)(2,1)}, s16[272,128]{1,0:T(8,128)(2,1)S(1)}, u32[]{:S(2)}, u32[]{:S(2)}) collective-permute-start(s16[272,128]{1,0:T(8,128)(2,1)} %get-tuple-element.41), channel_id=1, source_target_pairs={{0,1},{1,2},{2,3},{3,0},{4,5},{5,6},{6,7},{7,4},{8,9},{9,10},{10,1... | collective-permute-start | bytes 208904 | tf_op jit(solution)/shard_map/ppermute | solution.py:478
  5.7 11.9 %collective-permute-start.1 = (s16[272,128]{1,0:T(8,128)(2,1)}, s16[272,128]{1,0:T(8,128)(2,1)S(1)}, u32[]{:S(2)}, u32[]{:S(2)}) collective-permute-start(s16[272,128]{1,0:T(8,128)(2,1)} %get-tuple-element.42), channel_id=1, source_target_pairs={{0,2},{1,3},{2,0},{3,1},{4,6},{5,7},{6,4},{7,5},{8,10},{9,11},{10,... | collective-permute-start | bytes 208904 | tf_op jit(solution)/shard_map/ppermute | solution.py:478
  9.0 8.6 %collective-permute-start.2 = (s16[272,128]{1,0:T(8,128)(2,1)}, s16[272,128]{1,0:T(8,128)(2,1)S(1)}, u32[]{:S(2)}, u32[]{:S(2)}) collective-permute-start(s16[272,128]{1,0:T(8,128)(2,1)} %get-tuple-element.43), channel_id=1, source_target_pairs={{0,3},{1,0},{2,1},{3,2},{4,7},{5,4},{6,5},{7,6},{8,11},{9,8},{10,9... | collective-permute-start | bytes 208904 | tf_op jit(solution)/shard_map/ppermute | solution.py:478
  9.7 30.3 %collective-permute-start.4 = (bf16[32,64,256]{2,1,0:T(8,128)(2,1)}, bf16[32,64,256]{2,1,0:T(8,128)(2,1)}, u32[]{:S(2)}, u32[]{:S(2)}) collective-permute-start(bf16[32,64,256]{2,1,0:T(8,128)(2,1)} %bitcast.2.current), channel_id=1, source_target_pairs={{4,8},{8,4},{12,16},{16,12},{20,24},{24,20},{28,32},{32,28},{36,40... | collective-permute-start | bytes 3145736 | tf_op jit(solution)/shard_map/ppermute | solution.py:510
  14.3 25.7 %collective-permute-start.3 = (bf16[32,64,256]{2,1,0:T(8,128)(2,1)}, bf16[32,64,256]{2,1,0:T(8,128)(2,1)}, u32[]{:S(2)}, u32[]{:S(2)}) collective-permute-start(bf16[32,64,256]{2,1,0:T(8,128)(2,1)} %bitcast.2.current), channel_id=1, source_target_pairs={{4,0},{0,4},{12,8},{8,12},{20,16},{16,20},{28,24},{24,28},{36,32},... | collective-permute-start | bytes 3145736 | tf_op jit(solution)/shard_map/ppermute | solution.py:509
  17.6 0.9 %copy-start = (s16[272,128]{1,0:T(8,128)(2,1)S(1)}, s16[272,128]{1,0:T(8,128)(2,1)}, u32[]{:S(2)}) copy-start(s16[272,128]{1,0:T(8,128)(2,1)} %get-tuple-element.51.r0.m0) | copy-start | bytes 208900
  18.5 21.5 %copy-start.1 = (s16[272,128]{1,0:T(8,128)(2,1)S(1)}, s16[272,128]{1,0:T(8,128)(2,1)}, u32[]{:S(2)}) copy-start(s16[272,128]{1,0:T(8,128)(2,1)} %get-tuple-element.51.r0.m0) | copy-start | bytes 208900
  18.5 21.5 %copy-start.7 = (s32[64,8]{0,1:T(8,128)S(1)}, s32[64,8]{0,1:T(8,128)}, u32[]{:S(2)}) copy-start(s32[64,8]{0,1:T(8,128)} %param.30) | copy-start | bytes 6148
  18.5 21.5 %copy-start.8 = (s32[64,8]{0,1:T(8,128)S(1)}, s32[64,8]{0,1:T(8,128)}, u32[]{:S(2)}) copy-start(s32[64,8]{0,1:T(8,128)} %param.31) | copy-start | bytes 6148
  23.8 16.3 %all-to-all-start = ((f32[32,16,128]{2,1,0:T(8,128)}), f32[32,16,128]{2,1,0:T(8,128)S(1)}, u32[]{:S(2)}, u32[]{:S(2)}) async-start(f32[32,16,128]{2,1,0:T(8,128)} %get-tuple-element.59), calls=%async_computation | async-start | bytes 524288 | tf_op jit(solution)/shard_map/all_to_all | solution.py:572
  31.0 24.3 %collective-permute-start.5 = (s16[1040,128]{1,0:T(8,128)(2,1)S(1)}, s16[1040,128]{1,0:T(8,128)(2,1)S(1)}, u32[]{:S(2)}, u32[]{:S(2)}) collective-permute-start(s16[1040,128]{1,0:T(8,128)(2,1)S(1)} %get-tuple-element.62), channel_id=1, source_target_pairs={{0,1},{1,2},{2,3},{3,0},{4,5},{5,6},{6,7},{7,4},{8,9},{9,10},{10,1... | collective-permute-start | bytes 798728 | tf_op jit(solution)/shard_map/ppermute | solution.py:478
  31.8 23.5 %collective-permute-start.6 = (s16[1040,128]{1,0:T(8,128)(2,1)S(1)}, s16[1040,128]{1,0:T(8,128)(2,1)S(1)}, u32[]{:S(2)}, u32[]{:S(2)}) collective-permute-start(s16[1040,128]{1,0:T(8,128)(2,1)S(1)} %get-tuple-element.63), channel_id=1, source_target_pairs={{0,2},{1,3},{2,0},{3,1},{4,6},{5,7},{6,4},{7,5},{8,10},{9,11},{10,... | collective-permute-start | bytes 798728 | tf_op jit(solution)/shard_map/ppermute | solution.py:478
  32.0 23.4 %collective-permute-start.7 = (s16[1040,128]{1,0:T(8,128)(2,1)S(1)}, s16[1040,128]{1,0:T(8,128)(2,1)S(1)}, u32[]{:S(2)}, u32[]{:S(2)}) collective-permute-start(s16[1040,128]{1,0:T(8,128)(2,1)S(1)} %get-tuple-element.64), channel_id=1, source_target_pairs={{0,3},{1,0},{2,1},{3,2},{4,7},{5,4},{6,5},{7,6},{8,11},{9,8},{10,9... | collective-permute-start | bytes 798728 | tf_op jit(solution)/shard_map/ppermute | solution.py:478
  40.0 15.3 %copy-start.4 = (s32[8,8]{1,0:T(8,128)S(1)}, s32[8,8]{1,0:T(8,128)}, u32[]{:S(2)}) copy-start(s32[8,8]{1,0:T(8,128)} %kinds_from.1) | copy-start | bytes 772
  40.1 15.3 %copy-start.5 = (s32[8,8]{1,0:T(8,128)S(1)}, s32[8,8]{1,0:T(8,128)}, u32[]{:S(2)}) copy-start(s32[8,8]{1,0:T(8,128)} %lists_from.1) | copy-start | bytes 772
  43.5 13.1 %all-to-all-start.1 = ((f32[32,16,128]{2,1,0:T(8,128)}), f32[32,16,128]{2,1,0:T(8,128)S(1)}, u32[]{:S(2)}, u32[]{:S(2)}) async-start(f32[32,16,128]{2,1,0:T(8,128)} %bitcast.4), calls=%async_computation.1 | async-start | bytes 524288 | tf_op jit(solution)/shard_map/all_to_all | solution.py:595
  47.2 8.2 %collective-permute-start.9 = (bf16[128,512]{1,0:T(8,128)(2,1)S(1)}, bf16[128,512]{1,0:T(8,128)(2,1)S(1)}, u32[]{:S(2)}, u32[]{:S(2)}) collective-permute-start(bf16[128,512]{1,0:T(8,128)(2,1)S(1)} %get-tuple-element.65), channel_id=1, source_target_pairs={{4,8},{8,4},{12,16},{16,12},{20,24},{24,20},{28,32},{32,28},{36,40... | collective-permute-start | bytes 393224 | tf_op jit(solution)/shard_map/ppermute | solution.py:574
  50.7 4.6 %collective-permute-start.8 = (bf16[128,512]{1,0:T(8,128)(2,1)S(1)}, bf16[128,512]{1,0:T(8,128)(2,1)S(1)}, u32[]{:S(2)}, u32[]{:S(2)}) collective-permute-start(bf16[128,512]{1,0:T(8,128)(2,1)S(1)} %get-tuple-element.65), channel_id=1, source_target_pairs={{4,0},{0,4},{12,8},{8,12},{20,16},{16,20},{28,24},{24,28},{36,32},... | collective-permute-start | bytes 393224 | tf_op jit(solution)/shard_map/ppermute | solution.py:573
  60.4 11.0 %collective-permute-start.12 = (s16[528,128]{1,0:T(8,128)(2,1)S(1)}, s16[528,128]{1,0:T(8,128)(2,1)S(1)}, u32[]{:S(2)}, u32[]{:S(2)}) collective-permute-start(s16[528,128]{1,0:T(8,128)(2,1)S(1)} %lower.1.l0), channel_id=1, source_target_pairs={{0,3},{1,0},{2,1},{3,2},{4,7},{5,4},{6,5},{7,6},{8,11},{9,8},{10,9... | collective-permute-start | bytes 405512 | tf_op jit(solution)/shard_map/ppermute | solution.py:478
  60.5 10.9 %collective-permute-start.11 = (s16[528,128]{1,0:T(8,128)(2,1)S(1)}, s16[528,128]{1,0:T(8,128)(2,1)S(1)}, u32[]{:S(2)}, u32[]{:S(2)}) collective-permute-start(s16[528,128]{1,0:T(8,128)(2,1)S(1)} %lower.1.l0), channel_id=1, source_target_pairs={{0,2},{1,3},{2,0},{3,1},{4,6},{5,7},{6,4},{7,5},{8,10},{9,11},{10,... | collective-permute-start | bytes 405512 | tf_op jit(solution)/shard_map/ppermute | solution.py:478
  63.0 8.4 %collective-permute-start.10 = (s16[528,128]{1,0:T(8,128)(2,1)S(1)}, s16[528,128]{1,0:T(8,128)(2,1)S(1)}, u32[]{:S(2)}, u32[]{:S(2)}) collective-permute-start(s16[528,128]{1,0:T(8,128)(2,1)S(1)} %lower.1.l0), channel_id=1, source_target_pairs={{0,1},{1,2},{2,3},{3,0},{4,5},{5,6},{6,7},{7,4},{8,9},{9,10},{10,1... | collective-permute-start | bytes 405512 | tf_op jit(solution)/shard_map/ppermute | solution.py:478

commit v3 on v1

--- a/solution.py
+++ b/solution.py
@@ -12,20 +12,19 @@
 I32 = jnp.int32
 I16 = jnp.int16
 IN_HBM = pl.BlockSpec(memory_space=pltpu.HBM)
-IN_VMEM = pl.BlockSpec(memory_space=pltpu.VMEM)
 ANYWHERE = pl.BlockSpec(memory_space=pl.ANY)
 MIB = 1024 * 1024
 SMALL = 2**12
 LARGE = 2**36
 
 
-def call(kernel, outs, operands, scratch, copies, cost, name, landed=(), limit=52, kept=()):
+def call(kernel, outs, operands, scratch, copies, cost, name, landed=(), limit=52):
     shapes = tuple(jax.ShapeDtypeStruct(shape, kind) for shape, kind in outs)
     return pl.pallas_call(
         kernel,
         out_shape=shapes,
         in_specs=[ANYWHERE if n in landed else IN_HBM for n in range(len(operands))],
-        out_specs=tuple(IN_VMEM if n in kept else IN_HBM for n in range(len(outs))),
+        out_specs=tuple(IN_HBM for _ in outs),
         scratch_shapes=[*scratch, pltpu.SemaphoreType.DMA((copies,))],
         compiler_params=pltpu.CompilerParams(vmem_limit_bytes=limit * MIB),
         cost_estimate=pl.CostEstimate(flops=cost, bytes_accessed=cost, transcendentals=0),
@@ -305,26 +304,27 @@
 
 
 def parent_kernel(
-    kinds_from, lists_from, before_from, parent_from, after_from, m0, m1, m2, m3,
+    kinds_from, lists_from, inner_from, parent_from, outer_from, m0, m1, m2, m3,
     out_to,
-    kinds, lists, before, after, held, codes, table, out, sems,
+    kinds, lists, inner, outer, held, codes, table, out, sems,
 ):
     finish(
         *begin(
             sems,
             (kinds_from, kinds),
             (lists_from, lists),
-            (before_from, before),
+            (inner_from, inner),
             (parent_from, held.at[8:16]),
-            (after_from, after),
+            (outer_from, outer),
             *[(m.at[176:272], codes.at[sender(k)]) for k, m in enumerate((m0, m1, m2, m3))],
         )
     )
     base = lax.axis_index("space") * 8 - 8
     for e in range(4):
         table[e] = value_of(codes[e, 0:80]) * unit_from(value_of(codes[e, 80:96])[2:3])
-    held[0:8] = before[...].astype(F32).reshape(8, 2, 8, 512)
-    held[16:24] = after[...].astype(F32).reshape(8, 2, 8, 512)
+    odd = lax.rem(lax.axis_index("space"), 2)
+    held[pl.ds(16 - 16 * odd, 8)] = inner[...].astype(F32).reshape(8, 2, 8, 512)
+    held[pl.ds(16 * odd, 8)] = outer[...].astype(F32).reshape(8, 2, 8, 512)
 
     def body(p, carry):
         re = [jnp.zeros((8, 128), F32) for _ in range(4)]
@@ -404,17 +404,15 @@
     finish(*begin(sems, (out, out_to)))
 
 
-def near_kernel(half, lists_from, counts_from, before, current, after, blocks_from, out_to, lists, counts, held, blocks, out, sems):
-    if half == 0:
-        sources = [(before, held.at[0:32]), (after.at[0:16], held.at[64:80])]
-    else:
-        sources = [(before.at[16:32], held.at[16:32]), (after, held.at[64:96])]
+def near_kernel(half, lists_from, counts_from, inner, current, outer, blocks_from, out_to, lists, counts, held, blocks, out, sems):
+    odd = lax.rem(lax.axis_index("space"), 2)
     copies = begin(
         sems,
         (lists_from, lists),
         (counts_from, counts),
+        (inner, held.at[pl.ds(64 - 64 * odd, 32)]),
         (current, held.at[32:64]),
-        *sources,
+        (outer, held.at[pl.ds(64 * odd, 32)]),
         *[
             (blocks_from.at[16 * half + 4 * t : 16 * half + 4 * t + 4], blocks.at[4 * t : 4 * t + 4])
             for t in range(4)
@@ -531,12 +529,12 @@
 ):
     n_space = lax.axis_size("space")
     n_dir = lax.axis_size("dir")
-    up = [(i, i + 1) for i in range(n_space - 1)]
-    down = [(i + 1, i) for i in range(n_space - 1)]
+    first_swap = [(i ^ 1, i) for i in range(n_space)]
+    second_swap = [(i, j) for k in range(1, n_space - 1, 2) for i, j in ((k, k + 1), (k + 1, k))]
 
     flat = currents.reshape(32, 64, 256)
-    before = lax.ppermute(flat, "space", up)
-    after = lax.ppermute(flat, "space", down)
+    inner = lax.ppermute(flat, "space", first_swap)
+    outer = lax.ppermute(flat, "space", second_swap)
 
     leaf = call(
         leaf_kernel,
@@ -553,8 +551,7 @@
         6,
         LARGE,
         "leaf",
-        limit=60,
-        kept=(0,),
+        limit=62,
     )
     own_leaf = leaf[0]
     leaf = [own_leaf] + [around(leaf[k], "dir", n_dir, k) for k in (1, 2, 3)]
@@ -575,7 +572,7 @@
         "pack",
     )
     packed, angles = packed[:4], packed[4:]
-    leaf, packed, before, after = lax.optimization_barrier((leaf, packed, before, after))
+    leaf, packed = lax.optimization_barrier((leaf, packed))
     packed = [packed[0]] + [around(packed[k], "dir", n_dir, k) for k in (1, 2, 3)]
 
 
@@ -597,13 +594,13 @@
         16,
         LARGE,
         "lift",
-        landed=(0, 1, 2, 3),
+        landed=(1, 2, 3),
     )
     top = lax.all_to_all(message, "space", 0, 0)
-    parents_before = lax.ppermute(halo, "space", up)
-    parents_after = lax.ppermute(halo, "space", down)
-
-    top, parents_before, parents_after = lax.optimization_barrier((top, parents_before, parents_after))
+    parents_inner = lax.ppermute(halo, "space", first_swap)
+    parents_outer = lax.ppermute(halo, "space", second_swap)
+
+    top, inner, outer = lax.optimization_barrier((top, inner, outer))
     (moved,) = call(
         top_kernel,
         [((64, 8, 128), F32)],
@@ -620,15 +617,17 @@
         7,
         LARGE,
         "translate_two",
-        landed=(2, 3, 4, 5, 6),
-    )
+        landed=(2, 4, 5, 6),
+    )
+    moved, parents_inner, parents_outer = lax.optimization_barrier((moved, parents_inner, parents_outer))
     arrived = lax.all_to_all(moved.reshape(32, 16, 128), "space", 0, 0)
 
-    near_parts = [near_half(half, near_list.T, near_count, before, flat, after, near_blocks) for half in (0, 1)]
+    packed, parents_inner, parents_outer = lax.optimization_barrier((packed, parents_inner, parents_outer))
+    near_parts = [near_half(half, near_list.T, near_count, inner, flat, outer, near_blocks) for half in (0, 1)]
     (near_one,) = call(
         parent_kernel,
         [((8, 2, 8, 512), F32)],
-        [kind_one, list_one, parents_before, parent, parents_after] + leaf,
+        [kind_one, list_one, parents_inner, parent, parents_outer] + leaf,
         [
             pltpu.SMEM((8, 8), I32),
             pltpu.SMEM((8, 8), I32),
@@ -642,7 +641,7 @@
         9,
         SMALL,
         "translate_one",
-        landed=(2, 4, 5, 6, 7, 8),
+        landed=(2, 4, 6, 7, 8),
     )
 
     arrived, near_one, near_parts[0] = lax.optimization_barrier((arrived, near_one, near_parts[0]))

time: 87.1 us -> 75.5 us (0.87)
  starting transfers between devices: 43.8 us -> 34.5 us
  local copies, waits for them, and re-layouts: 1.87 us -> 0.92 us
    ppermute x4, starting transfers between devices: 12.2 us -> 8.36 us  [the longest x1 3.44 us: shards(): parents_outer = lax.ppermute(halo, 'space', second_swap)]
    all_to_all x1, starting transfers between devices: 8.77 us -> 4.92 us  [shards(): arrived = lax.all_to_all(moved.reshape(32, 16, 128), 'space', 0, 0)]
    ppermute x4, waiting for transfers between devices: 2.49 us -> 0.01 us  [the longest x1 0.01 us: shards(): outer = lax.ppermute(flat, 'space', second_swap)]
    all_to_all x1, starting transfers between devices: 9.02 us -> 6.91 us  [shards(): top = lax.all_to_all(message, 'space', 0, 0)]
    all_to_all x1, waiting for transfers between devices: 0.01 us -> 1.64 us  [shards(): arrived = lax.all_to_all(moved.reshape(32, 16, 128), 'space', 0, 0)]
    all_to_all x1, waiting for transfers between devices: 0.92 us -> 1.94 us  [shards(): top = lax.all_to_all(message, 'space', 0, 0)]
    unnamed x20, local copies, waits for them, and re-layouts: 1.87 us -> 0.92 us
  transfers between devices with their start and end apart: 15 -> 15, of which waited for: 3 -> 3; matrix products, arithmetic and copies ran while one was open for 0% -> 0% of each run, Pallas kernels for 27% -> 33%
where the time goes in v3:
time: 75.5 us; the launch traced here: 75.1 us
  Pallas kernels  35.4 us (47%)
  starting transfers between devices  34.5 us (46%)
  waiting for transfers between devices  3.93 us (5%)
  local copies, waits for them, and re-layouts  0.92 us (1%)
    pallas_call x9, Pallas kernels, call(): pl.pallas_call(kernel, out_shape=shapes, in_specs=[ANYWHERE if n in lande...  35.4 us
    ppermute x9, starting transfers between devices, around(): return lax.ppermute(x, axis, [(i, (i + k) % peers) for i in range(peers)])  14.3 us
    all_to_all x1, starting transfers between devices, shards(): top = lax.all_to_all(message, 'space', 0, 0)  6.91 us
    all_to_all x1, starting transfers between devices, shards(): arrived = lax.all_to_all(moved.reshape(32, 16, 128), 'space', 0, 0)  4.92 us
    ppermute x1, starting transfers between devices, shards(): parents_outer = lax.ppermute(halo, 'space', second_swap)  3.44 us
    ppermute x1, starting transfers between devices, shards(): outer = lax.ppermute(flat, 'space', second_swap)  3.08 us
    all_to_all x1, waiting for transfers between devices, shards(): top = lax.all_to_all(message, 'space', 0, 0)  1.94 us
    all_to_all x1, waiting for transfers between devices, shards(): arrived = lax.all_to_all(moved.reshape(32, 16, 128), 'space', 0, 0)  1.64 us
  transfers between devices with their start and end apart: 15, of which 3 were waited for; matrix products, arithmetic and copies ran while one was open for 0% of the time, Pallas kernels for 33%

profile of v3, /device:TPU:1, one launch (start us, length us, event | category | flops | bytes accessed | tf_op | source)
XLA Modules:
  0.0 75.1 jit_solution(9678669797648806709)
XLA Ops:
  0.0 3.2 %leaf.1 = (s16[272,128]{1,0:T(8,128)(2,1)}, s16[272,128]{1,0:T(8,128)(2,1)}, s16[272,128]{1,0:T(8,128)(2,1)}, s16[272,128]{1,0:T(8,128)(2,1)}) custom-call(bf16[32,2,32,256]{3,2,1,0:T(8,128)(2,1)} %cur_from.1, bf16[32,2,32,256]{3,2,1,0:T(8,128)(2,1)} %rad_from.1, f32[40,2,128]{2,1,0:T(2,128)} %one_from.1, f32[40,2,512]{2,1,0:T(2,128)} %two_from.1), custom_call_target="tpu_custom_call" | custom-call | flops 68719476736 | bytes 68719476736 | tf_op jit(solution)/shard_map/leaf/pallas_call | solution.py:23
  3.2 2.5 %collective-permute-start = (s16[272,128]{1,0:T(8,128)(2,1)}, s16[272,128]{1,0:T(8,128)(2,1)S(1)}, u32[]{:S(2)}, u32[]{:S(2)}) collective-permute-start(s16[272,128]{1,0:T(8,128)(2,1)} %get-tuple-element.47), channel_id=1, source_target_pairs={{0,1},{1,2},{2,3},{3,0},{4,5},{5,6},{6,7},{7,4},{8,9},{9,10},{10,1... | collective-permute-start | bytes 208904 | tf_op jit(solution)/shard_map/ppermute | solution.py:505
  5.7 3.3 %collective-permute-start.1 = (s16[272,128]{1,0:T(8,128)(2,1)}, s16[272,128]{1,0:T(8,128)(2,1)S(1)}, u32[]{:S(2)}, u32[]{:S(2)}) collective-permute-start(s16[272,128]{1,0:T(8,128)(2,1)} %get-tuple-element.48), channel_id=1, source_target_pairs={{0,2},{1,3},{2,0},{3,1},{4,6},{5,7},{6,4},{7,5},{8,10},{9,11},{10,... | collective-permute-start | bytes 208904 | tf_op jit(solution)/shard_map/ppermute | solution.py:505
  9.0 0.7 collective-permute-start.2
  9.7 1.5 %collective-permute-start.3 = (bf16[32,64,256]{2,1,0:T(8,128)(2,1)}, bf16[32,64,256]{2,1,0:T(8,128)(2,1)}, u32[]{:S(2)}, u32[]{:S(2)}) collective-permute-start(bf16[32,64,256]{2,1,0:T(8,128)(2,1)} %bitcast.2.current), channel_id=1, source_target_pairs={{4,0},{0,4},{12,8},{8,12},{20,16},{16,20},{28,24},{24,28},{36,32},... | collective-permute-start | bytes 3145736 | tf_op jit(solution)/shard_map/ppermute | solution.py:536
  11.3 3.1 %collective-permute-start.4 = (bf16[32,64,256]{2,1,0:T(8,128)(2,1)}, bf16[32,64,256]{2,1,0:T(8,128)(2,1)}, u32[]{:S(2)}, u32[]{:S(2)}) collective-permute-start(bf16[32,64,256]{2,1,0:T(8,128)(2,1)} %bitcast.2.current), channel_id=1, source_target_pairs={{4,8},{8,4},{12,16},{16,12},{20,24},{24,20},{28,32},{32,28},{36,40... | collective-permute-start | bytes 3145736 | tf_op jit(solution)/shard_map/ppermute | solution.py:537
  14.4 3.1 %pack.1 = (s16[1040,128]{1,0:T(8,128)(2,1)S(1)}, s16[1040,128]{1,0:T(8,128)(2,1)S(1)}, s16[1040,128]{1,0:T(8,128)(2,1)S(1)}, s16[1040,128]{1,0:T(8,128)(2,1)S(1)...) custom-call(f32[32,2,32,256]{3,2,1,0:T(8,128)} %rec_from, ...), custom_call_target="tpu_custom_call" | custom-call | flops 4096 | bytes 4096 | tf_op jit(solution)/shard_map/pack/pallas_call | solution.py:23
  17.5 0.9 %copy-done = s16[272,128]{1,0:T(8,128)(2,1)S(1)} copy-done((s16[272,128]{1,0:T(8,128)(2,1)S(1)}, s16[272,128]{1,0:T(8,128)(2,1)}, u32[]{:S(2)}) %copy-start) | copy-done | bytes 69656
  18.4 5.3 %lift.1 = (f32[8,2,8,512]{3,2,1,0:T(8,128)S(1)}, bf16[128,512]{1,0:T(8,128)(2,1)S(1)}, f32[32,16,128]{2,1,0:T(8,128)}) custom-call(s16[272,128]{1,0:T(8,128)(2,1)S(1)} %copy-done, s16[272,128]{1,0:T(8,128)(2,1)S(1)} %collective-permute-done.r1.m1, s16[272,128]{1,0:T(8,128)(2,1)S(1)} %collective-permute-done.1.r2.m2, ...), custom_call_target="tpu_custom_call" | custom-call | flops 68719476736 | bytes 68719476736 | tf_op jit(solution)/shard_map/lift/pallas_call | solution.py:23
  23.7 6.9 %all-to-all-start = ((f32[32,16,128]{2,1,0:T(8,128)}), f32[32,16,128]{2,1,0:T(8,128)S(1)}, u32[]{:S(2)}, u32[]{:S(2)}) async-start(f32[32,16,128]{2,1,0:T(8,128)} %get-tuple-element.65), calls=%async_computation | async-start | bytes 524288 | tf_op jit(solution)/shard_map/all_to_all | solution.py:599
  30.9 3.4 %collective-permute-start.6 = (bf16[128,512]{1,0:T(8,128)(2,1)S(1)}, bf16[128,512]{1,0:T(8,128)(2,1)S(1)}, u32[]{:S(2)}, u32[]{:S(2)}) collective-permute-start(bf16[128,512]{1,0:T(8,128)(2,1)S(1)} %get-tuple-element.67), channel_id=1, source_target_pairs={{4,8},{8,4},{12,16},{16,12},{20,24},{24,20},{28,32},{32,28},{36,40... | collective-permute-start | bytes 393224 | tf_op jit(solution)/shard_map/ppermute | solution.py:601
  34.4 0.8 %collective-permute-start.7 = (s16[1040,128]{1,0:T(8,128)(2,1)S(1)}, s16[1040,128]{1,0:T(8,128)(2,1)S(1)}, u32[]{:S(2)}, u32[]{:S(2)}) collective-permute-start(s16[1040,128]{1,0:T(8,128)(2,1)S(1)} %get-tuple-element.70), channel_id=1, source_target_pairs={{0,1},{1,2},{2,3},{3,0},{4,5},{5,6},{6,7},{7,4},{8,9},{9,10},{10,1... | collective-permute-start | bytes 798728 | tf_op jit(solution)/shard_map/ppermute | solution.py:505
  35.3 2.3 %collective-permute-start.9 = (s16[1040,128]{1,0:T(8,128)(2,1)S(1)}, s16[1040,128]{1,0:T(8,128)(2,1)S(1)}, u32[]{:S(2)}, u32[]{:S(2)}) collective-permute-start(s16[1040,128]{1,0:T(8,128)(2,1)S(1)} %get-tuple-element.72), channel_id=1, source_target_pairs={{0,3},{1,0},{2,1},{3,2},{4,7},{5,4},{6,5},{7,6},{8,11},{9,8},{10,9... | collective-permute-start | bytes 798728 | tf_op jit(solution)/shard_map/ppermute | solution.py:505
  37.7 1.9 %all-to-all-done = f32[32,16,128]{2,1,0:T(8,128)S(1)} async-done(((f32[32,16,128]{2,1,0:T(8,128)}), f32[32,16,128]{2,1,0:T(8,128)S(1)}, u32[]{:S(2)}, u32[]{:S(2)}) %all-to-all-start) | async-done | bytes 262176 | tf_op jit(solution)/shard_map/all_to_all | solution.py:599
  39.6 3.4 %translate_two.1 = f32[64,8,128]{2,1,0:T(8,128)} custom-call(s32[8,64]{1,0:T(8,128)S(1)} %bitcast.7, s32[8,64]{1,0:T(8,128)S(1)} %bitcast.8, f32[64,8,128]{2,1,0:T(8,128)S(1)} %bitcast.6, s16[272,128]{1,0:T(8,128)(2,1)S(1)} %copy-done.1, s16[272,128]{1,0:T(8,128)(2,1)S(1)} %collective-permute-done.r1.m1, s16[272,128]{1,0:T(8,128)(2,1)S(1)} %collective-permute-done.1.r2.m2, ...), custom_call_target="tpu_custom_call" | custom-call | flops 68719476736 | bytes 68719476736 | tf_op jit(solution)/shard_map/translate_two/pallas_call | solution.py:23
  43.0 4.9 %all-to-all-start.1 = ((f32[32,16,128]{2,1,0:T(8,128)}), f32[32,16,128]{2,1,0:T(8,128)S(1)}, u32[]{:S(2)}, u32[]{:S(2)}) async-start(f32[32,16,128]{2,1,0:T(8,128)} %bitcast.4), calls=%async_computation.1 | async-start | bytes 524288 | tf_op jit(solution)/shard_map/all_to_all | solution.py:623
  48.3 1.2 %translate_one.1.near_one_from = f32[8,2,8,512]{3,2,1,0:T(8,128)S(1)} custom-call(s32[8,8]{1,0:T(8,128)S(1)} %copy-done.4, s32[8,8]{1,0:T(8,128)S(1)} %copy-done.5, bf16[128,512]{1,0:T(8,128)(2,1)S(1)} %collective-permute-done.5.inner_from, f32[8,2,8,512]{3,2,1,0:T(8,128)S(1)} %get-tuple-element.76.parent_from, ...), custom_call_target="tpu_custom_call" | custom-call | flops 4096 | bytes 4096 | tf_op jit(solution)/shard_map/translate_one/pallas_call | solution.py:23
  49.5 5.8 %near.2.near_first = f32[16,64,128]{2,1,0:T(8,128)} custom-call(s32[6,32]{1,0:T(8,128)} %bitcast.9, s32[32]{0:T(128)} %counts_from.3, bf16[32,64,256]{2,1,0:T(8,128)(2,1)} %collective-permute-done.3.inner, bf16[32,64,256]{2,1,0:T(8,128)(2,1)} %bitcast.2.current, bf16[32,64,256]{2,1,0:T(8,128)(2,1)} %collective-permute-done.4.outer, ...), custom_call_target="tpu_custom_call" | custom-call | flops 4096 | bytes 4096 | tf_op jit(solution)/shard_map/near/pallas_call | solution.py:23
  55.3 1.6 %all-to-all-done.1.arrived_from = f32[32,16,128]{2,1,0:T(8,128)S(1)} async-done(((f32[32,16,128]{2,1,0:T(8,128)}), f32[32,16,128]{2,1,0:T(8,128)S(1)}, u32[]{:S(2)}, u32[]{:S(2)}) %all-to-all-start.1) | async-done | bytes 262176 | tf_op jit(solution)/shard_map/all_to_all | solution.py:623
  57.0 3.8 %lower.1.l0 = s16[528,128]{1,0:T(8,128)(2,1)S(1)} custom-call(f32[32,16,128]{2,1,0:T(8,128)S(1)} %all-to-all-done.1.arrived_from, f32[8,2,8,512]{3,2,1,0:T(8,128)S(1)} %translate_one.1.near_one_from, f32[4,512]{1,0:T(4,128)S(1)} %get-tuple-element.61.refs_2_.refs_0_, f32[4,512]{1,0:T(4,128)S(1)} %get-tuple-element.62.refs_3_.refs_1_, ...), custom_call_target="tpu_custom_call" | custom-call | flops 68719476736 | bytes 68719476736 | tf_op jit(solution)/shard_map/lower/pallas_call | solution.py:23
  61.1 2.2 %collective-permute-start.11 = (s16[528,128]{1,0:T(8,128)(2,1)S(1)}, s16[528,128]{1,0:T(8,128)(2,1)S(1)}, u32[]{:S(2)}, u32[]{:S(2)}) collective-permute-start(s16[528,128]{1,0:T(8,128)(2,1)S(1)} %lower.1.l0), channel_id=1, source_target_pairs={{0,2},{1,3},{2,0},{3,1},{4,6},{5,7},{6,4},{7,5},{8,10},{9,11},{10,... | collective-permute-start | bytes 405512 | tf_op jit(solution)/shard_map/ppermute | solution.py:505
  63.2 1.9 %collective-permute-start.12 = (s16[528,128]{1,0:T(8,128)(2,1)S(1)}, s16[528,128]{1,0:T(8,128)(2,1)S(1)}, u32[]{:S(2)}, u32[]{:S(2)}) collective-permute-start(s16[528,128]{1,0:T(8,128)(2,1)S(1)} %lower.1.l0), channel_id=1, source_target_pairs={{0,3},{1,0},{2,1},{3,2},{4,7},{5,4},{6,5},{7,6},{8,11},{9,8},{10,9... | collective-permute-start | bytes 405512 | tf_op jit(solution)/shard_map/ppermute | solution.py:505
  65.2 5.7 %near.3.near_second = f32[16,64,128]{2,1,0:T(8,128)} custom-call(s32[6,32]{1,0:T(8,128)} %bitcast.10, s32[32]{0:T(128)} %counts_from.3, bf16[32,64,256]{2,1,0:T(8,128)(2,1)} %collective-permute-done.3.inner, bf16[32,64,256]{2,1,0:T(8,128)(2,1)} %bitcast.2.current, bf16[32,64,256]{2,1,0:T(8,128)(2,1)} %collective-permute-done.4.outer, ...), custom_call_target="tpu_custom_call" | custom-call | flops 4096 | bytes 4096 | tf_op jit(solution)/shard_map/near/pallas_call | solution.py:23
  71.0 4.0 %receive.1 = f32[32,2,32,64]{3,2,1,0:T(8,128)} custom-call(s16[528,128]{1,0:T(8,128)(2,1)S(1)} %lower.1.l0, s16[528,128]{1,0:T(8,128)(2,1)S(1)} %collective-permute-done.10.l1, s16[528,128]{1,0:T(8,128)(2,1)S(1)} %collective-permute-done.11.l2, s16[528,128]{1,0:T(8,128)(2,1)S(1)} %collective-permute-done.12.l3, s16[1040,128]{1,0:T(8,128)(2,1)S(1)} %get-tuple-element.82.x0, ...), custom_call_target="tpu_custom_call" | custom-call | flops 68719476736 | bytes 68719476736 | tf_op jit(solution)/shard_map/receive/pallas_call | solution.py:23
  (35 shorter events, 1.2 us)
Async XLA Ops:
  0.0 14.4 %copy-start.3 = (f32[4,512]{1,0:T(4,128)S(1)}, f32[4,512]{1,0:T(4,128)}, u32[]{:S(2)}) copy-start(f32[4,512]{1,0:T(4,128)} %one_from.2) | copy-start | bytes 24580
  0.0 14.4 %copy-start.2 = (f32[4,2048]{1,0:T(4,128)S(1)}, f32[4,2048]{1,0:T(4,128)}, u32[]{:S(2)}) copy-start(f32[4,2048]{1,0:T(4,128)} %two_from.2) | copy-start | bytes 98308
  0.0 17.5 %copy-start.6 = (f32[512,128]{1,0:T(8,128)S(1)}, f32[512,128]{1,0:T(8,128)}, u32[]{:S(2)}) copy-start(f32[512,128]{1,0:T(8,128)} %refs_4_.1) | copy-start | bytes 786436
  3.2 14.3 %collective-permute-start = (s16[272,128]{1,0:T(8,128)(2,1)}, s16[272,128]{1,0:T(8,128)(2,1)S(1)}, u32[]{:S(2)}, u32[]{:S(2)}) collective-permute-start(s16[272,128]{1,0:T(8,128)(2,1)} %get-tuple-element.47), channel_id=1, source_target_pairs={{0,1},{1,2},{2,3},{3,0},{4,5},{5,6},{6,7},{7,4},{8,9},{9,10},{10,1... | collective-permute-start | bytes 208904 | tf_op jit(solution)/shard_map/ppermute | solution.py:505
  5.7 11.8 %collective-permute-start.1 = (s16[272,128]{1,0:T(8,128)(2,1)}, s16[272,128]{1,0:T(8,128)(2,1)S(1)}, u32[]{:S(2)}, u32[]{:S(2)}) collective-permute-start(s16[272,128]{1,0:T(8,128)(2,1)} %get-tuple-element.48), channel_id=1, source_target_pairs={{0,2},{1,3},{2,0},{3,1},{4,6},{5,7},{6,4},{7,5},{8,10},{9,11},{10,... | collective-permute-start | bytes 208904 | tf_op jit(solution)/shard_map/ppermute | solution.py:505
  9.0 8.5 %collective-permute-start.2 = (s16[272,128]{1,0:T(8,128)(2,1)}, s16[272,128]{1,0:T(8,128)(2,1)S(1)}, u32[]{:S(2)}, u32[]{:S(2)}) collective-permute-start(s16[272,128]{1,0:T(8,128)(2,1)} %get-tuple-element.49), channel_id=1, source_target_pairs={{0,3},{1,0},{2,1},{3,2},{4,7},{5,4},{6,5},{7,6},{8,11},{9,8},{10,9... | collective-permute-start | bytes 208904 | tf_op jit(solution)/shard_map/ppermute | solution.py:505
  9.7 25.4 %collective-permute-start.3 = (bf16[32,64,256]{2,1,0:T(8,128)(2,1)}, bf16[32,64,256]{2,1,0:T(8,128)(2,1)}, u32[]{:S(2)}, u32[]{:S(2)}) collective-permute-start(bf16[32,64,256]{2,1,0:T(8,128)(2,1)} %bitcast.2.current), channel_id=1, source_target_pairs={{4,0},{0,4},{12,8},{8,12},{20,16},{16,20},{28,24},{24,28},{36,32},... | collective-permute-start | bytes 3145736 | tf_op jit(solution)/shard_map/ppermute | solution.py:536
  11.3 24.1 %collective-permute-start.4 = (bf16[32,64,256]{2,1,0:T(8,128)(2,1)}, bf16[32,64,256]{2,1,0:T(8,128)(2,1)}, u32[]{:S(2)}, u32[]{:S(2)}) collective-permute-start(bf16[32,64,256]{2,1,0:T(8,128)(2,1)} %bitcast.2.current), channel_id=1, source_target_pairs={{4,8},{8,4},{12,16},{16,12},{20,24},{24,20},{28,32},{32,28},{36,40... | collective-permute-start | bytes 3145736 | tf_op jit(solution)/shard_map/ppermute | solution.py:537
  18.4 21.2 %copy-start.1 = (s16[272,128]{1,0:T(8,128)(2,1)S(1)}, s16[272,128]{1,0:T(8,128)(2,1)}, u32[]{:S(2)}) copy-start(s16[272,128]{1,0:T(8,128)(2,1)} %get-tuple-element.57.r0.m0) | copy-start | bytes 208900
  18.4 21.2 %copy-start.8 = (s32[64,8]{0,1:T(8,128)S(1)}, s32[64,8]{0,1:T(8,128)}, u32[]{:S(2)}) copy-start(s32[64,8]{0,1:T(8,128)} %param.30) | copy-start | bytes 6148
  18.4 21.2 %copy-start.9 = (s32[64,8]{0,1:T(8,128)S(1)}, s32[64,8]{0,1:T(8,128)}, u32[]{:S(2)}) copy-start(s32[64,8]{0,1:T(8,128)} %param.31) | copy-start | bytes 6148
  23.7 15.9 %all-to-all-start = ((f32[32,16,128]{2,1,0:T(8,128)}), f32[32,16,128]{2,1,0:T(8,128)S(1)}, u32[]{:S(2)}, u32[]{:S(2)}) async-start(f32[32,16,128]{2,1,0:T(8,128)} %get-tuple-element.65), calls=%async_computation | async-start | bytes 524288 | tf_op jit(solution)/shard_map/all_to_all | solution.py:599
  30.6 12.4 %collective-permute-start.5 = (bf16[128,512]{1,0:T(8,128)(2,1)S(1)}, bf16[128,512]{1,0:T(8,128)(2,1)S(1)}, u32[]{:S(2)}, u32[]{:S(2)}) collective-permute-start(bf16[128,512]{1,0:T(8,128)(2,1)S(1)} %get-tuple-element.67), channel_id=1, source_target_pairs={{4,0},{0,4},{12,8},{8,12},{20,16},{16,20},{28,24},{24,28},{36,32},... | collective-permute-start | bytes 393224 | tf_op jit(solution)/shard_map/ppermute | solution.py:600
  30.9 12.1 %collective-permute-start.6 = (bf16[128,512]{1,0:T(8,128)(2,1)S(1)}, bf16[128,512]{1,0:T(8,128)(2,1)S(1)}, u32[]{:S(2)}, u32[]{:S(2)}) collective-permute-start(bf16[128,512]{1,0:T(8,128)(2,1)S(1)} %get-tuple-element.67), channel_id=1, source_target_pairs={{4,8},{8,4},{12,16},{16,12},{20,24},{24,20},{28,32},{32,28},{36,40... | collective-permute-start | bytes 393224 | tf_op jit(solution)/shard_map/ppermute | solution.py:601
  34.4 13.6 %collective-permute-start.7 = (s16[1040,128]{1,0:T(8,128)(2,1)S(1)}, s16[1040,128]{1,0:T(8,128)(2,1)S(1)}, u32[]{:S(2)}, u32[]{:S(2)}) collective-permute-start(s16[1040,128]{1,0:T(8,128)(2,1)S(1)} %get-tuple-element.70), channel_id=1, source_target_pairs={{0,1},{1,2},{2,3},{3,0},{4,5},{5,6},{6,7},{7,4},{8,9},{9,10},{10,1... | collective-permute-start | bytes 798728 | tf_op jit(solution)/shard_map/ppermute | solution.py:505
  35.2 12.8 %collective-permute-start.8 = (s16[1040,128]{1,0:T(8,128)(2,1)S(1)}, s16[1040,128]{1,0:T(8,128)(2,1)S(1)}, u32[]{:S(2)}, u32[]{:S(2)}) collective-permute-start(s16[1040,128]{1,0:T(8,128)(2,1)S(1)} %get-tuple-element.71), channel_id=1, source_target_pairs={{0,2},{1,3},{2,0},{3,1},{4,6},{5,7},{6,4},{7,5},{8,10},{9,11},{10,... | collective-permute-start | bytes 798728 | tf_op jit(solution)/shard_map/ppermute | solution.py:505
  35.3 13.0 %collective-permute-start.9 = (s16[1040,128]{1,0:T(8,128)(2,1)S(1)}, s16[1040,128]{1,0:T(8,128)(2,1)S(1)}, u32[]{:S(2)}, u32[]{:S(2)}) collective-permute-start(s16[1040,128]{1,0:T(8,128)(2,1)S(1)} %get-tuple-element.72), channel_id=1, source_target_pairs={{0,3},{1,0},{2,1},{3,2},{4,7},{5,4},{6,5},{7,6},{8,11},{9,8},{10,9... | collective-permute-start | bytes 798728 | tf_op jit(solution)/shard_map/ppermute | solution.py:505
  39.6 8.7 %copy-start.4 = (s32[8,8]{1,0:T(8,128)S(1)}, s32[8,8]{1,0:T(8,128)}, u32[]{:S(2)}) copy-start(s32[8,8]{1,0:T(8,128)} %kinds_from.1) | copy-start | bytes 772
  39.6 8.7 %copy-start.5 = (s32[8,8]{1,0:T(8,128)S(1)}, s32[8,8]{1,0:T(8,128)}, u32[]{:S(2)}) copy-start(s32[8,8]{1,0:T(8,128)} %lists_from.1) | copy-start | bytes 772
  43.0 13.9 %all-to-all-start.1 = ((f32[32,16,128]{2,1,0:T(8,128)}), f32[32,16,128]{2,1,0:T(8,128)S(1)}, u32[]{:S(2)}, u32[]{:S(2)}) async-start(f32[32,16,128]{2,1,0:T(8,128)} %bitcast.4), calls=%async_computation.1 | async-start | bytes 524288 | tf_op jit(solution)/shard_map/all_to_all | solution.py:623
  49.5 7.4 %copy-start.7 = (f32[512,128]{1,0:T(8,128)S(1)}, f32[512,128]{1,0:T(8,128)}, u32[]{:S(2)}) copy-start(f32[512,128]{1,0:T(8,128)} %refs_4_.1) | copy-start | bytes 786436
  60.8 10.2 %collective-permute-start.10 = (s16[528,128]{1,0:T(8,128)(2,1)S(1)}, s16[528,128]{1,0:T(8,128)(2,1)S(1)}, u32[]{:S(2)}, u32[]{:S(2)}) collective-permute-start(s16[528,128]{1,0:T(8,128)(2,1)S(1)} %lower.1.l0), channel_id=1, source_target_pairs={{0,1},{1,2},{2,3},{3,0},{4,5},{5,6},{6,7},{7,4},{8,9},{9,10},{10,1... | collective-permute-start | bytes 405512 | tf_op jit(solution)/shard_map/ppermute | solution.py:505
  61.1 9.9 %collective-permute-start.11 = (s16[528,128]{1,0:T(8,128)(2,1)S(1)}, s16[528,128]{1,0:T(8,128)(2,1)S(1)}, u32[]{:S(2)}, u32[]{:S(2)}) collective-permute-start(s16[528,128]{1,0:T(8,128)(2,1)S(1)} %lower.1.l0), channel_id=1, source_target_pairs={{0,2},{1,3},{2,0},{3,1},{4,6},{5,7},{6,4},{7,5},{8,10},{9,11},{10,... | collective-permute-start | bytes 405512 | tf_op jit(solution)/shard_map/ppermute | solution.py:505
  63.2 7.7 %collective-permute-start.12 = (s16[528,128]{1,0:T(8,128)(2,1)S(1)}, s16[528,128]{1,0:T(8,128)(2,1)S(1)}, u32[]{:S(2)}, u32[]{:S(2)}) collective-permute-start(s16[528,128]{1,0:T(8,128)(2,1)S(1)} %lower.1.l0), channel_id=1, source_target_pairs={{0,3},{1,0},{2,1},{3,2},{4,7},{5,4},{6,5},{7,6},{8,11},{9,8},{10,9... | collective-permute-start | bytes 405512 | tf_op jit(solution)/shard_map/ppermute | solution.py:505
  (1 other events, 0.9 us)
